TPU v7x, 32 devices: a whole 2x2x4 slice. The times are simulated.
32 devices in a mesh: dp: 4 (over z), ep: 8 (over y, x, core).
Axes of the slice: x: 2, y: 2, z: 4, core: 2. Of those that a mesh axis runs over, the one named last changes fastest.
Arguments:
- tokens: bfloat16 [8192, 1024], P(('dp', 'ep')), may hold values from -6 to 6
- gain_attn: float32 [1024], replicated, may hold values from 0.5 to 1.5
- shift_attn: float32 [1024], replicated, may hold values from -1.5 to 1.5
- w_qkv: bfloat16 [1024, 3072], replicated, may hold values from -0.1875 to 0.1875
- w_o: bfloat16 [1024, 1024], replicated, may hold values from -3 to 3
- gain_ffn: float32 [1024], replicated, may hold values from 0.5 to 1.5
- shift_ffn: float32 [1024], replicated, may hold values from -1.5 to 1.5
- w_in: bfloat16 [8, 4096, 1024], P('ep'), may hold values from -0.1875 to 0.1875
- w_out: bfloat16 [8, 4096, 1024], P('ep'), may hold values from -0.1875 to 0.1875
- seq_lengths: int32 [4, 4], P('dp'), may hold values from 1 to 1920, as said below
- expert_ids: int32 [8192, 1], P(('dp', 'ep')), may hold values from 0 to 7; in each aligned block of 256 rows (0 to 255, 256 to 511, ...) at most 64 rows name the same one
- cotangent: bfloat16 [8192, 1024], P(('dp', 'ep')), may hold values from -6 to 6
Outputs:
- block_out: bfloat16 [8192, 1024], P(('dp', 'ep'))
- grad_tokens: float32 [8192, 1024], P(('dp', 'ep'))
- grad_w_qkv: float32 [1024, 3072], replicated
- grad_w_o: float32 [1024, 1024], replicated
- grad_gain_attn: float32 [1024], replicated
- grad_shift_attn: float32 [1024], replicated
- grad_gain_ffn: float32 [1024], replicated
- grad_shift_ffn: float32 [1024], replicated
- grad_w_in: float32 [8, 4096, 1024], P('ep', 'dp')
- grad_w_out: float32 [8, 4096, 1024], P('ep', 'dp')
Inputs may be any that keep to these rules, and one draw needn't show every extreme that they name: `seq_lengths`: each group holds 4 sequences that fill its 2048 tokens; the second is 1920 tokens long and the others are shorter, each 1 or more. `expert_ids`: of the 256 rows of one device at most 64 name the same expert; in some such blocks one expert is named by exactly 64.
All inputs are finite; a program needn't handle non-finite values.
Results may differ from a plain program's by a relative error of at most 0.03.
Values may be sent and summed in bfloat16 or wider, within the bound.
A program may use at most 320 MiB of HBM per device.

v0:
```python
import jax
import jax.numpy as jnp
from jax import lax
from jax.sharding import PartitionSpec as P

HEADS = 16


EPSILON = 1e-05
MASKED = -1e30


def norm_forward(rows_in, gain_vec, shift_vec):
    average = jnp.mean(rows_in, axis=-1, keepdims=True)
    centered = rows_in - average
    inv_std = lax.rsqrt(jnp.mean(centered * centered, axis=-1, keepdims=True) + EPSILON)
    unit_rows = centered * inv_std
    return (unit_rows * gain_vec + shift_vec, unit_rows, inv_std)


def norm_backward(grad_rows, unit_rows, inv_std, gain_vec):
    grad_unit = grad_rows * gain_vec
    grad_in = inv_std * (
        grad_unit
        - jnp.mean(grad_unit, axis=-1, keepdims=True)
        - unit_rows * jnp.mean(grad_unit * unit_rows, axis=-1, keepdims=True)
    )
    return (grad_in, jnp.sum(grad_rows * unit_rows, axis=0), jnp.sum(grad_rows, axis=0))


def sequence_starts(lengths, positions):
    ends_at = jnp.cumsum(lengths)
    starts_at = ends_at - lengths
    return jnp.max(
        jnp.where(starts_at[None, :] <= positions[:, None], starts_at[None, :], 0), axis=1
    )


def visible(key_pos, query_pos, query_start):
    return (key_pos[None, :] <= query_pos[:, None]) & (key_pos[None, :] >= query_start[:, None])


def contract_rows(left, right):
    return lax.dot_general(
        left, right, (((0,), (0,)), ((), ())), preferred_element_type=jnp.float32
    )


def contract_cols(left, right):
    return lax.dot_general(
        left, right, (((1,), (1,)), ((), ())), preferred_element_type=jnp.float32
    )


def attention_probs(query_heads, key_heads, allowed, log_total, score_scale):
    scores = (
        jnp.einsum("qhd,khd->hqk", query_heads, key_heads, preferred_element_type=jnp.float32)
        * score_scale
    )
    scores = jnp.where(allowed[None], scores, MASKED)
    return jnp.where(allowed[None], jnp.exp(scores - log_total[:, :, None]), 0.0)


def on_device(
    tokens,
    gain_attn,
    shift_attn,
    w_qkv,
    w_o,
    gain_ffn,
    shift_ffn,
    w_in,
    w_out,
    seq_lengths,
    expert_ids,
    cotangent,
):
    tok_rows, model_width = tokens.shape
    head_count = HEADS
    head_size = model_width // head_count
    score_scale = head_size ** (-0.5)
    lengths = seq_lengths[0]
    my_first = lax.axis_index("ep") * tok_rows
    positions = my_first + jnp.arange(tok_rows, dtype=jnp.int32)
    query_starts = sequence_starts(lengths, positions)
    lowest = query_starts[0]
    highest = positions[-1]
    inputs = tokens.astype(jnp.float32)
    normed, unit_attn, inv_attn = norm_forward(inputs, gain_attn, shift_attn)
    normed_low = normed.astype(jnp.bfloat16)
    qkv = jnp.dot(normed_low, w_qkv, preferred_element_type=jnp.float32).astype(jnp.bfloat16)
    query_flat = qkv[:, :model_width]
    key_rows = qkv[:, model_width : 2 * model_width]
    value_rows = qkv[:, 2 * model_width :]
    queries = query_flat.reshape(tok_rows, head_count, head_size)
    start_fold = (
        jnp.full((head_count, tok_rows), MASKED, jnp.float32),
        jnp.zeros((head_count, tok_rows), jnp.float32),
        jnp.zeros((tok_rows, head_count, head_size), jnp.float32),
    )
    first_row = jnp.int32(0)
    key_part = lax.all_gather(key_rows, "ep", axis=0, tiled=True)
    value_part = lax.all_gather(value_rows, "ep", axis=0, tiled=True)
    piece_rows = key_part.shape[0]

    def forward_compute(running):
        running_max, running_sum, accum = running
        key_pos = jnp.arange(piece_rows, dtype=jnp.int32)
        allowed = visible(key_pos, positions, query_starts)[None]
        scores = (
            jnp.einsum(
                "qhd,khd->hqk",
                queries,
                key_part.reshape(piece_rows, head_count, head_size),
                preferred_element_type=jnp.float32,
            )
            * score_scale
        )
        scores = jnp.where(allowed, scores, MASKED)
        new_max = jnp.maximum(running_max, jnp.max(scores, axis=-1))
        weights = jnp.where(allowed, jnp.exp(scores - new_max[:, :, None]), 0.0)
        decay = jnp.exp(running_max - new_max)
        new_sum = jnp.sum(weights, axis=-1)
        update = jnp.einsum(
            "hqk,khd->qhd",
            weights.astype(jnp.bfloat16),
            value_part.reshape(piece_rows, head_count, head_size),
            preferred_element_type=jnp.float32,
        )
        return (new_max, new_sum, accum * decay.T[:, :, None] + update)

    needed = (first_row <= highest) & (first_row + piece_rows - 1 >= lowest)
    running_max, running_sum, accum = lax.cond(
        needed, forward_compute, lambda running: running, start_fold
    )
    attended = accum / running_sum.T[:, :, None]
    log_total = running_max + jnp.log(running_sum)
    attended_low = attended.reshape(tok_rows, model_width).astype(jnp.bfloat16)
    hidden_res = inputs + jnp.dot(attended_low, w_o, preferred_element_type=jnp.float32)
    routed, unit_ffn, inv_ffn = norm_forward(hidden_res, gain_ffn, shift_ffn)
    routed_low = routed.astype(jnp.bfloat16)
    experts_total = lax.axis_size("ep")
    capacity = 2 * tok_rows // experts_total
    chosen_ids = expert_ids[:, 0]
    one_hot = (chosen_ids[:, None] == jnp.arange(experts_total, dtype=jnp.int32)[None, :]).astype(
        jnp.int32
    )
    slot_of = jnp.sum((jnp.cumsum(one_hot, axis=0) - 1) * one_hot, axis=1)
    target = chosen_ids * capacity + slot_of
    placing = (
        jnp.arange(experts_total * capacity, dtype=jnp.int32)[:, None] == target[None, :]
    ).astype(jnp.bfloat16)
    outbound = jnp.dot(placing, routed_low, preferred_element_type=jnp.float32).astype(jnp.bfloat16)
    outbound = outbound.reshape(experts_total, capacity, model_width)
    weight_in = w_in[0]
    weight_out = w_out[0]
    arrived = lax.all_to_all(outbound, "ep", split_axis=0, concat_axis=0, tiled=True)
    flat_rows = arrived.reshape(-1, model_width)
    pre_act = contract_cols(flat_rows, weight_in)
    activated = jax.nn.gelu(pre_act, approximate=True).astype(jnp.bfloat16)
    produced = jnp.dot(activated, weight_out, preferred_element_type=jnp.float32).astype(
        jnp.bfloat16
    )
    returned = lax.all_to_all(
        produced.reshape(arrived.shape), "ep", split_axis=0, concat_axis=0, tiled=True
    )
    expert_rows = contract_rows(placing, returned.reshape(-1, model_width))
    block_out = (hidden_res + expert_rows).astype(jnp.bfloat16)
    grad_outbound = jnp.dot(placing, cotangent, preferred_element_type=jnp.float32).astype(
        jnp.bfloat16
    )
    grad_received = lax.all_to_all(
        grad_outbound.reshape(experts_total, capacity, model_width),
        "ep",
        split_axis=0,
        concat_axis=0,
        tiled=True,
    )
    flat_in = arrived.reshape(-1, model_width)
    flat_grad = grad_received.reshape(-1, model_width)
    pre_act = contract_cols(flat_in, weight_in)
    act_low = jax.nn.gelu(pre_act, approximate=True).astype(jnp.bfloat16)
    grad_act = contract_cols(flat_grad, weight_out)
    _, gelu_pull = jax.vjp(lambda inner: jax.nn.gelu(inner, approximate=True), pre_act)
    grad_pre = gelu_pull(grad_act)[0].astype(jnp.bfloat16)
    grad_rows = jnp.dot(grad_pre, weight_in, preferred_element_type=jnp.float32).astype(
        jnp.bfloat16
    )
    grad_back = lax.all_to_all(
        grad_rows.reshape(experts_total, capacity, model_width),
        "ep",
        split_axis=0,
        concat_axis=0,
        tiled=True,
    )
    grad_routed = contract_rows(placing, grad_back.reshape(-1, model_width))
    expert_grads = lax.psum_scatter(
        jnp.concatenate(
            [contract_rows(grad_pre, flat_in), contract_rows(act_low, flat_grad)], axis=1
        ).astype(jnp.bfloat16),
        "dp",
        scatter_dimension=0,
        tiled=True,
    ).astype(jnp.float32)
    grad_normed2, grad_gain_ffn, grad_shift_ffn = norm_backward(
        grad_routed, unit_ffn, inv_ffn, gain_ffn
    )
    grad_hidden = cotangent.astype(jnp.float32) + grad_normed2
    grad_hidden_low = grad_hidden.astype(jnp.bfloat16)
    grad_w_o = contract_rows(attended_low, grad_hidden_low)
    grad_att_low = (
        contract_cols(grad_hidden_low, w_o)
        .astype(jnp.bfloat16)
        .reshape(tok_rows, head_count, head_size)
    )
    delta = jnp.sum(grad_att_low.astype(jnp.float32) * attended, axis=-1).T
    group_rows = tok_rows * lax.axis_size("ep")
    zero_queries = jnp.zeros((tok_rows, head_count, head_size), jnp.float32)
    zero_group = jnp.zeros((group_rows, model_width), jnp.float32)
    back_init = (zero_queries, zero_group, zero_group)
    first_row = jnp.int32(0)
    backward_key_part = lax.all_gather(key_rows, "ep", axis=0, tiled=True)
    backward_value_part = lax.all_gather(value_rows, "ep", axis=0, tiled=True)
    backward_piece_rows = backward_key_part.shape[0]

    def backward_compute(running):
        key_pos = jnp.arange(backward_piece_rows, dtype=jnp.int32)
        key_heads = backward_key_part.reshape(backward_piece_rows, head_count, head_size)
        value_heads = backward_value_part.reshape(backward_piece_rows, head_count, head_size)
        allowed = visible(key_pos, positions, query_starts)
        softmax_w = attention_probs(queries, key_heads, allowed, log_total, score_scale)
        grad_probs = jnp.einsum(
            "qhd,khd->hqk", grad_att_low, value_heads, preferred_element_type=jnp.float32
        )
        grad_scores = (softmax_w * (grad_probs - delta[:, :, None])).astype(jnp.bfloat16)
        grad_q = score_scale * jnp.einsum(
            "hqk,khd->qhd", grad_scores, key_heads, preferred_element_type=jnp.float32
        )
        new_keys = score_scale * jnp.einsum(
            "hqk,qhd->khd", grad_scores, queries, preferred_element_type=jnp.float32
        )
        new_values = jnp.einsum(
            "hqk,qhd->khd",
            softmax_w.astype(jnp.bfloat16),
            grad_att_low,
            preferred_element_type=jnp.float32,
        )
        sum_keys = new_keys.reshape(backward_piece_rows, model_width)
        sum_values = new_values.reshape(backward_piece_rows, model_width)
        return (grad_q, sum_keys, sum_values)

    needed = (first_row <= highest) & (first_row + backward_piece_rows - 1 >= lowest)
    back_fold = lax.cond(needed, backward_compute, lambda running: running, back_init)
    grad_queries = back_fold[0].reshape(tok_rows, model_width)
    grad_keys, grad_values = (
        lax.psum_scatter(
            back_fold[1].astype(jnp.bfloat16), "ep", scatter_dimension=0, tiled=True
        ).astype(jnp.float32),
        lax.psum_scatter(
            back_fold[2].astype(jnp.bfloat16), "ep", scatter_dimension=0, tiled=True
        ).astype(jnp.float32),
    )
    grad_qkv = jnp.concatenate(
        [
            grad_queries.astype(jnp.bfloat16),
            grad_keys.astype(jnp.bfloat16),
            grad_values.astype(jnp.bfloat16),
        ],
        axis=1,
    )
    grad_w_qkv = contract_rows(normed_low, grad_qkv)
    grad_normed1 = contract_cols(grad_qkv, w_qkv)
    grad_in1, grad_gain_attn, grad_shift_attn = norm_backward(
        grad_normed1, unit_attn, inv_attn, gain_attn
    )
    grad_tokens = grad_hidden + grad_in1
    summed = lax.psum(
        (grad_w_qkv, grad_w_o, grad_gain_attn, grad_shift_attn, grad_gain_ffn, grad_shift_ffn),
        ("dp", "ep"),
    )
    grad_w_in = expert_grads[:, :model_width][None]
    grad_w_out = expert_grads[:, model_width:][None]
    return (
        block_out,
        grad_tokens,
        summed[0],
        summed[1],
        summed[2],
        summed[3],
        summed[4],
        summed[5],
        grad_w_in,
        grad_w_out,
    )


def solution(mesh):
    return jax.shard_map(
        on_device,
        mesh=mesh,
        in_specs=(
            P(("dp", "ep"), None),
            P(),
            P(),
            P(),
            P(),
            P(),
            P(),
            P("ep", None, None),
            P("ep", None, None),
            P("dp", None),
            P(("dp", "ep"), None),
            P(("dp", "ep"), None),
        ),
        out_specs=(
            P(("dp", "ep"), None),
            P(("dp", "ep"), None),
            P(),
            P(),
            P(),
            P(),
            P(),
            P(),
            P("ep", "dp", None),
            P("ep", "dp", None),
        ),
        check_vma=False,
    )
```

profile of v0, /device:TPU:0, one launch (start us, length us, event | category | flops | bytes accessed | tf_op | source)
XLA Modules:
  0.0 1043.2 jit_solution(7587983699121783520)
XLA Ops:
  21.5 34.1 %all-gather.3.cloned.1.call-done = bf16[2048,1024]{1,0:T(8,128)(2,1)} async-done(((bf16[256,1024]{1,0:T(8,128)(2,1)}), bf16[2048,1024]{1,0:T(8,128)(2,1)}) %all-gather.3.cloned.1.call-update) | async-done | bytes 4194320 | tf_op jit(solution)/shard_map/all_gather | solution.py:102
  55.6 39.2 %all-gather.5.cloned.1.call-done = bf16[2048,1024]{1,0:T(8,128)(2,1)} async-done(((bf16[256,1024]{1,0:T(8,128)(2,1)}), bf16[2048,1024]{1,0:T(8,128)(2,1)}) %all-gather.5.cloned.1.call-update) | async-done | bytes 4194320 | tf_op jit(solution)/shard_map/all_gather | solution.py:103
  94.8 63.8 %conditional.2 = (f32[16,256]{1,0:T(8,128)}, f32[16,256]{1,0:T(8,128)}, f32[256,16,64]{0,2,1:T(8,128)S(1)}, f32[16,256]{1,0:T(8,128)S(1)}) conditional(s32[]{:T(128)} %bitcast.13, () %tuple.28, (s32[256]{0:T(256)S(1)}, s32[256]{0:T(256)S(1)}, bf16[2048,1024]{1,0:T(8,128)(2,1)}, bf16[256,16,64]{0,2,1:T(8,128)(2,1)}, bf16[2048,1024]{1,0:T(8,128)(2,1)}) %tuple.29), branch_computations={%region_4.5_spmd, %region_5.8_spmd} | conditional | flops 2258374656 | bytes 131762240 | solution.py:133
  95.9 6.6 copy.41
  102.5 15.3 %fusion = (f32[16,256]{1,0:T(8,128)S(1)}, f32[16,256,2048]{2,1,0:T(8,128)}) fusion(pred[256,2048]{1,0:T(8,128)(4,1)S(1)} %fusion.6, bf16[256,16,64]{0,2,1:T(8,128)(2,1)} %get-tuple-element.33, bf16[2048,16,64]{0,2,1:T(8,128)(2,1)} %bitcast.95), kind=kOutput, calls=%fused_computation.2 | convolution fusion | flops 1098903552 | bytes 38813696 | tf_op jit(solution)/shard_map/cond/branch_1_fun/qhd,khd->hqk/dot_general | solution.py:111
  118.5 6.4 copy.42
  124.9 16.7 %fusion.10 = f32[256,16,64]{0,2,1:T(8,128)S(1)} fusion(bf16[2048,16,64]{0,2,1:T(8,128)(2,1)} %bitcast.99, f32[16,256,2048]{2,1,0:T(8,128)} %get-tuple-element.158, f32[16,256]{1,0:T(8,128)} %get-tuple-element.174, pred[256,2048]{1,0:T(8,128)(4,1)} %copy-done.9, f32[256,16]{0,1:T(8,128)S(1)} %get-tuple-element.155), kind=kOutput, calls=%fused_computation.11 | convolution fusion | flops 1115947008 | bytes 39354368 | tf_op jit(solution)/shard_map/cond/branch_1_fun/hqk,khd->qhd/dot_general | solution.py:124
  141.6 16.3 %fusion.2 = f32[16,256]{1,0:T(8,128)} fusion(f32[16,256,2048]{2,1,0:T(8,128)} %get-tuple-element.158, f32[16,256]{1,0:T(8,128)} %get-tuple-element.174, pred[256,2048]{1,0:T(8,128)(4,1)} %copy-done.9), kind=kLoop, calls=%fused_computation.4 | loop fusion | flops 41938944 | bytes 34111488 | tf_op jit(solution)/shard_map/cond/branch_1_fun/reduce_sum | solution.py:123
  171.2 13.0 %all-to-all-done = bf16[8,64,1024]{2,1,0:T(8,128)(2,1)} async-done(((bf16[8,64,1024]{2,1,0:T(8,128)(2,1)}), bf16[8,64,1024]{2,1,0:T(8,128)(2,1)}, u32[]{:S(2)}, u32[]{:S(2)}) %all-to-all-start) | async-done | bytes 1048608 | tf_op jit(solution)/shard_map/all_to_all | solution.py:157
  188.4 11.5 %fusion.38 = f32[512,4096]{1,0:T(8,128)} fusion(bf16[512,1024]{1,0:T(8,128)(2,1)} %bitcast.22, bf16[1,4096,1024]{2,1,0:T(8,128)(2,1)} %param.23), kind=kOutput, calls=%fused_computation.47 | convolution fusion | flops 4294967296 | bytes 17825792 | tf_op jit(solution)/shard_map/dot_general | solution.py:50
  203.8 12.6 %fusion.31 = bf16[512,4096]{1,0:T(8,128)(2,1)S(1)} fusion(f32[512,4096]{1,0:T(8,128)} %fusion.38, bf16[512,1024]{1,0:T(8,128)(2,1)} %bitcast.28, bf16[1,4096,1024]{2,1,0:T(8,128)(2,1)} %param.24), kind=kOutput, calls=%fused_computation.40 | convolution fusion | flops 4336910336 | bytes 22020096 | tf_op jit(solution)/shard_map/dot_general | solution.py:50
  216.5 9.6 fusion.40
  231.0 14.8 %all-to-all-done.3 = bf16[8,64,1024]{2,1,0:T(8,128)(2,1)} async-done(((bf16[8,64,1024]{2,1,0:T(8,128)(2,1)}), bf16[8,64,1024]{2,1,0:T(8,128)(2,1)}, u32[]{:S(2)}, u32[]{:S(2)}) %all-to-all-start.3) | async-done | bytes 1048608 | tf_op jit(solution)/shard_map/all_to_all | solution.py:189
  253.2 92.7 %conditional.3 = (bf16[2048,1024]{0,1:T(8,128)(2,1)}, bf16[2048,1024]{0,1:T(8,128)(2,1)}, bf16[256,1024]{0,1:T(8,128)(2,1)S(1)}) conditional(s32[]{:T(128)} %bitcast.13, () %tuple.30, (s32[256]{0:T(256)S(1)}, s32[256]{0:T(256)S(1)}, bf16[2048,1024]{1,0:T(8,128)(2,1)}, bf16[256,16,64]{0,2,1:T(8,128)(2,1)}, f32[16,256]{1,0:T(8,128)}, ...), branch_computations={%region_16.17_spmd, %region_17.18_spmd} | conditional | flops 5475667968 | bytes 209815616 | solution.py:253
  253.4 6.4 copy.44
  259.8 17.9 %fusion.83 = f32[16,256,2048]{2,1,0:T(8,128)} fusion(bf16[256,16,64]{0,2,1:T(8,128)(2,1)} %get-tuple-element.38, bf16[2048,16,64]{0,2,1:T(8,128)(2,1)} %bitcast.93), kind=kOutput, calls=%fused_computation.127 | convolution fusion | flops 1073741824 | bytes 38273024 | tf_op jit(solution)/shard_map/cond/branch_1_fun/qhd,khd->hqk/dot_general | solution.py:57
  285.7 23.5 %multiply_convert_fusion = bf16[16,256,2048]{2,1,0:T(8,128)(2,1)} fusion(f32[16,256,2048]{2,1,0:T(8,128)} %fusion.83, bf16[256,16,64]{0,2,1:T(8,128)(2,1)S(1)} %get-tuple-element.42, bf16[2048,16,64]{0,2,1:T(8,128)(2,1)} %bitcast.100, f32[16,256]{1,0:T(8,128)S(1)} %get-tuple-element.44, f32[16,256]{1,0:T(8,128)S(1)} %add.84, pred[256,2048]{1,0:T(8,128)(4,1)S(1)} %fusion.20), kind=kOutput, calls=%fused_computation.17 | convolution fusion | flops 1132462080 | bytes 55607296 | tf_op jit(solution)/shard_map/cond/branch_1_fun/qhd,khd->hqk/dot_general | solution.py:232
  309.2 9.0 fusion.21
  318.2 11.0 %convolution_multiply_fusion = bf16[16,2048,64]{1,2,0:T(8,128)(2,1)} fusion(bf16[256,16,64]{0,2,1:T(8,128)(2,1)} %get-tuple-element.38, bf16[16,256,2048]{2,1,0:T(8,128)(2,1)} %multiply_convert_fusion), kind=kOutput, calls=%fused_computation.22 | convolution fusion | flops 1077936128 | bytes 21495808 | tf_op jit(solution)/shard_map/cond/branch_1_fun/hqk,qhd->khd/dot_general | solution.py:239
  329.2 16.4 %fusion.17 = bf16[16,2048,64]{1,2,0:T(8,128)(2,1)} fusion(bf16[256,16,64]{0,2,1:T(8,128)(2,1)S(1)} %get-tuple-element.42, f32[16,256,2048]{2,1,0:T(8,128)} %fusion.83, f32[16,256]{1,0:T(8,128)S(1)} %add.84, pred[256,2048]{1,0:T(8,128)(4,1)S(1)} %fusion.20), kind=kOutput, calls=%fused_computation.20 | convolution fusion | flops 1115684864 | bytes 38813696 | tf_op jit(solution)/shard_map/cond/branch_1_fun/hqk,qhd->khd/dot_general | solution.py:242
  346.5 7.0 convolution_convert_fusion.1
  353.6 8.1 convolution_convert_fusion
  361.7 7.2 pad_maximum_fusion
  373.1 23.4 %reduce-scatter.4.cloned.1.call-done = bf16[256,1024]{0,1:T(8,128)(2,1)} async-done(((bf16[2048,1024]{0,1:T(8,128)(2,1)}), bf16[256,1024]{0,1:T(8,128)(2,1)}) %reduce-scatter.4.cloned.1.call-update) | async-done | bytes 524304 | tf_op jit(solution)/shard_map/reduce_scatter | solution.py:256
  398.4 53.7 %reduce-scatter.6.cloned.1.call-done = bf16[256,1024]{0,1:T(8,128)(2,1)} async-done(((bf16[2048,1024]{0,1:T(8,128)(2,1)}), bf16[256,1024]{0,1:T(8,128)(2,1)}) %reduce-scatter.6.cloned.1.call-update) | async-done | bytes 524304 | tf_op jit(solution)/shard_map/reduce_scatter | solution.py:259
  454.0 8.4 fusion.78
  462.4 11.1 %fusion.43 = bf16[512,1024]{1,0:T(8,128)(2,1)S(1)} fusion(bf16[1,4096,1024]{2,1,0:T(8,128)(2,1)} %param.24, f32[512,4096]{1,0:T(8,128)} %fusion.38), kind=kOutput, calls=%fused_computation.59 | convolution fusion | flops 4314365952 | bytes 17825792 | tf_op jit(solution)/shard_map/dot_general | solution.py:161
  473.5 17.9 %all_to_all.20 = bf16[8,64,1024]{2,1,0:T(8,128)(2,1)S(1)} all-to-all(bf16[8,64,1024]{2,1,0:T(8,128)(2,1)S(1)} %bitcast.106), channel_id=1, replica_groups=mesh['dp'=4,'ep'=8] {'ep'}, dimensions={0} | all-to-all | bytes 2097152 | tf_op jit(solution)/shard_map/all_to_all | solution.py:164
  497.7 44.1 %all-reduce = (f32[1024]{0:T(1024)}, f32[1024]{0:T(1024)}, f32[1024]{0:T(1024)}, f32[1024]{0:T(1024)}) all-reduce(f32[1024]{0:T(1024)S(1)} %get-tuple-element.143, f32[1024]{0:T(1024)S(1)} %get-tuple-element.148, f32[1024]{0:T(1024)S(1)} %copy-done.25, f32[1024]{0:T(1024)S(1)} %copy-done.26), channel_id=1, replica_groups=mesh['dp'=4,'ep'=8] {'dp','ep'}, use_global_device_ids=true, to_apply=%region_25.26 | all-reduce | flops 4096 | bytes 32768 | tf_op jit(solution)/shard_map/psum | solution.py:277
  543.2 192.4 %reduce-scatter.8.cloned.1.call-done = bf16[1024,2048]{0,1:T(8,128)(2,1)} async-done(((bf16[4096,2048]{0,1:T(8,128)(2,1)}), bf16[1024,2048]{0,1:T(8,128)(2,1)}) %reduce-scatter.8.cloned.1.call-update) | async-done | bytes 4194320 | tf_op jit(solution)/shard_map/reduce_scatter | solution.py:197
  753.7 269.2 %all-reduce.4.cloned.1.call-done = (f32[1024,3072]{1,0:T(8,128)}, f32[1024,1024]{1,0:T(8,128)}) async-done(((f32[1024,3072]{1,0:T(8,128)}, f32[1024,1024]{1,0:T(8,128)}), (f32[1024,3072]{1,0:T(8,128)}, f32[1024,1024]{1,0:T(8,128)})) %all-reduce.4.cloned.1.call-update) | async-done | bytes 16777232 | tf_op jit(solution)/shard_map/psum | solution.py:277
  1023.0 11.1 %copy.66 = f32[1024,3072]{1,0:T(8,128)} copy(f32[1024,3072]{1,0:T(8,128)} %get-tuple-element.186) | data formatting | bytes 25165824
  (127 shorter events, 92.2 us)
Async XLA Ops:
  7.2 153.3 %copy-start = (bf16[1024,1024]{1,0:T(8,128)(2,1)S(1)}, bf16[1024,1024]{1,0:T(8,128)(2,1)}, u32[]{:S(2)}) copy-start(bf16[1024,1024]{1,0:T(8,128)(2,1)} %param.20) | copy-start | bytes 6291460
  7.2 48.4 %all-gather.3.cloned.1.call-start = ((), (), s32[]{:S(2)}) async-start(), calls=%async_computation.7 | async-start | bytes 4718592 | tf_op jit(solution)/shard_map/all_gather | solution.py:102
  8.6 6.3 copy-start.16
  9.9 8.5 copy-start.27
  9.9 10.5 %copy-start.23 = (s32[256,1]{0,1:T(1,128)S(1)}, s32[256,1]{0,1:T(1,128)}, u32[]{:S(2)}) copy-start(s32[256,1]{0,1:T(1,128)} %param.26) | copy-start | bytes 3076
  16.0 78.8 %all-gather.5.cloned.1.call-start = ((), (), s32[]{:S(2)}) async-start(), calls=%async_computation.8 | async-start | bytes 4718592 | tf_op jit(solution)/shard_map/all_gather | solution.py:103
  21.5 224.3 %copy-start.21 = (s32[256]{0:T(256)}, s32[256]{0:T(256)S(1)}, u32[]{:S(2)}) copy-start(s32[256]{0:T(256)S(1)} %multiply_add_fusion.1) | copy-start | bytes 3076
  94.8 67.8 %copy-start.18 = (f32[1024]{0:T(1024)S(1)}, f32[1024]{0:T(1024)}, u32[]{:S(2)}) copy-start(f32[1024]{0:T(1024)} %param.21) | copy-start | bytes 12292
  94.8 67.8 %copy-start.24 = (f32[1024]{0:T(1024)S(1)}, f32[1024]{0:T(1024)}, u32[]{:S(2)}) copy-start(f32[1024]{0:T(1024)} %param.22) | copy-start | bytes 12292
  95.9 22.0 %copy-start.9 = (pred[256,2048]{1,0:T(8,128)(4,1)}, pred[256,2048]{1,0:T(8,128)(4,1)S(1)}, u32[]{:S(2)}) copy-start(pred[256,2048]{1,0:T(8,128)(4,1)S(1)} %fusion.6) | copy-start | bytes 1572868 | tf_op jit(solution)/shard_map/cond
  162.3 86.1 %copy-start.3 = (f32[256,1024]{1,0:T(8,128)}, f32[256,1024]{1,0:T(8,128)S(1)}, u32[]{:S(2)}) copy-start(f32[256,1024]{1,0:T(8,128)S(1)} %get-tuple-element.165) | copy-start | bytes 3145732
  164.2 20.0 %all-to-all-start = ((bf16[8,64,1024]{2,1,0:T(8,128)(2,1)}), bf16[8,64,1024]{2,1,0:T(8,128)(2,1)}, u32[]{:S(2)}, u32[]{:S(2)}) async-start(bf16[8,64,1024]{2,1,0:T(8,128)(2,1)} %bitcast.102), calls=%async_computation | async-start | bytes 2097152 | tf_op jit(solution)/shard_map/all_to_all | solution.py:157
  184.2 19.7 %all-to-all-start.2 = ((bf16[8,64,1024]{2,1,0:T(8,128)(2,1)}), bf16[8,64,1024]{2,1,0:T(8,128)(2,1)}, u32[]{:S(2)}, u32[]{:S(2)}) async-start(bf16[8,64,1024]{2,1,0:T(8,128)(2,1)} %bitcast.101), calls=%async_computation.2 | async-start | bytes 2097152 | tf_op jit(solution)/shard_map/all_to_all | solution.py:172
  216.5 9.6 copy-start.28
  226.1 19.7 %all-to-all-start.3 = ((bf16[8,64,1024]{2,1,0:T(8,128)(2,1)}), bf16[8,64,1024]{2,1,0:T(8,128)(2,1)}, u32[]{:S(2)}, u32[]{:S(2)}) async-start(bf16[8,64,1024]{2,1,0:T(8,128)(2,1)} %bitcast.105), calls=%async_computation.3 | async-start | bytes 2097152 | tf_op jit(solution)/shard_map/all_to_all | solution.py:189
  230.3 166.2 %reduce-scatter.4.cloned.1.call-start = ((), (), s32[]{:S(2)}) async-start(), calls=%async_computation.9 | async-start | bytes 4718592 | tf_op jit(solution)/shard_map/reduce_scatter | solution.py:256
  285.7 23.5 %copy-start.2 = (bf16[2048,1024]{0,1:T(8,128)(2,1)S(1)}, bf16[2048,1024]{0,1:T(8,128)(2,1)}, u32[]{:S(2)}) copy-start(bf16[2048,1024]{0,1:T(8,128)(2,1)} %copy.44) | copy-start | bytes 12582916 | tf_op jit(solution)/shard_map/cond
  345.9 106.2 %reduce-scatter.6.cloned.1.call-start = ((), (), s32[]{:S(2)}) async-start(), calls=%async_computation.10 | async-start | bytes 4718592 | tf_op jit(solution)/shard_map/reduce_scatter | solution.py:259
  346.5 389.1 %reduce-scatter.8.cloned.1.call-start = ((), (), s32[]{:S(2)}) async-start(), calls=%async_computation.11 | async-start | bytes 20971520 | tf_op jit(solution)/shard_map/reduce_scatter | solution.py:197
  368.9 85.0 %copy-start.7 = (bf16[256,1024]{1,0:T(8,128)(2,1)S(1)}, bf16[256,1024]{1,0:T(8,128)(2,1)}, u32[]{:S(2)}) copy-start(bf16[256,1024]{1,0:T(8,128)(2,1)} %param.16) | copy-start | bytes 1572868
  368.9 85.0 %copy-start.14 = (f32[1024]{0:T(1024)S(1)}, f32[1024]{0:T(1024)}, u32[]{:S(2)}) copy-start(f32[1024]{0:T(1024)} %param.17) | copy-start | bytes 12292
  369.0 85.0 %copy-start.15 = (f32[1024]{0:T(1024)S(1)}, f32[1024]{0:T(1024)}, u32[]{:S(2)}) copy-start(f32[1024]{0:T(1024)} %param.18) | copy-start | bytes 12292
  369.0 85.0 %copy-start.17 = (f32[256]{0:T(256)S(1)}, f32[256]{0:T(256)}, u32[]{:S(2)}) copy-start(f32[256]{0:T(256)} %copy-done.16) | copy-start | bytes 3076
  369.0 85.0 %copy-start.20 = (f32[256]{0:T(256)S(1)}, f32[256]{0:T(256)}, u32[]{:S(2)}) copy-start(f32[256]{0:T(256)} %copy-done.19) | copy-start | bytes 3076
  369.0 654.0 %all-reduce.4.cloned.1.call-start = ((), (), s32[]{:S(2)}) async-start(), calls=%async_computation.12 | async-start | bytes 33554432 | tf_op jit(solution)/shard_map/psum | solution.py:277
  462.4 29.0 %copy-start.4 = (f32[256,1024]{1,0:T(8,128)S(1)}, f32[256,1024]{1,0:T(8,128)}, u32[]{:S(2)}) copy-start(f32[256,1024]{1,0:T(8,128)} %copy-done.3) | copy-start | bytes 3145732
  462.4 29.0 %copy-start.22 = (s32[256]{0:T(256)S(1)}, s32[256]{0:T(256)}, u32[]{:S(2)}) copy-start(s32[256]{0:T(256)} %copy-done.21) | copy-start | bytes 3076
  462.4 30.2 %copy-start.13 = (bf16[256,3072]{0,1:T(8,128)(2,1)S(1)}, bf16[256,3072]{0,1:T(8,128)(2,1)}, u32[]{:S(2)}) copy-start(bf16[256,3072]{0,1:T(8,128)(2,1)} %constant_dynamic-update-slice_fusion) | copy-start | bytes 4718596
  473.5 24.2 %copy-start.25 = (f32[1024]{0:T(1024)S(1)}, f32[1024]{0:T(1024)}, u32[]{:S(2)}) copy-start(f32[1024]{0:T(1024)} %get-tuple-element.141) | copy-start | bytes 12292
  473.5 24.2 %copy-start.26 = (f32[1024]{0:T(1024)S(1)}, f32[1024]{0:T(1024)}, u32[]{:S(2)}) copy-start(f32[1024]{0:T(1024)} %get-tuple-element.147) | copy-start | bytes 12292
  1023.0 11.1 %copy-start.12 = (f32[1024,1024]{1,0:T(8,128)S(1)}, f32[1024,1024]{1,0:T(8,128)}, u32[]{:S(2)}) copy-start(f32[1024,1024]{1,0:T(8,128)} %get-tuple-element.187) | copy-start | bytes 12582916
  1023.0 13.2 %copy-start.1 = (bf16[1024,1024]{1,0:T(8,128)(2,1)S(1)}, bf16[1024,1024]{1,0:T(8,128)(2,1)}, u32[]{:S(2)}) copy-start(bf16[1024,1024]{1,0:T(8,128)(2,1)} %param.20) | copy-start | bytes 6291460
  (6 other events, 10.6 us)
Sparse Core Ops, SparseCore 0:
  16.2 39.4 all-gather.2
  58.1 36.7 all-gather.4
  346.0 50.4 reduce-scatter.3
  400.7 51.3 reduce-scatter.5
  454.3 281.2 reduce-scatter.7
  743.5 279.4 all-reduce.3
where the time goes:
time: 1050 us; the launch traced here: 1040 us
  waiting for transfers between devices  645 us (61%)
  matrix products  201 us (19%)
  local copies, waits for them, and re-layouts  65 us (6%)
  blocking collectives  62 us (6%)
  other arithmetic  38.6 us (4%)
  between operations  16 us (2%)
  starting transfers between devices  14.3 us (1%)
    psum x1, waiting for transfers between devices, on_device(): lax.psum((grad_w_qkv, grad_w_o, grad_gain_attn, grad_shift_attn, grad_gai...  269 us
    reduce_scatter x1, waiting for transfers between devices, on_device(): lax.psum_scatter(jnp.concatenate([contract_rows(grad_pre, flat_in), contr...  192 us
    reduce_scatter x1, waiting for transfers between devices, on_device(): lax.psum_scatter(back_fold[2].astype(jnp.bfloat16), 'ep', scatter_dimensi...  53.7 us
    psum x1, blocking collectives, on_device(): lax.psum((grad_w_qkv, grad_w_o, grad_gain_attn, grad_shift_attn, grad_gai...  44.1 us
    all_gather x1, waiting for transfers between devices, on_device(): value_part = lax.all_gather(value_rows, 'ep', axis=0, tiled=True)  39.2 us
    all_gather x1, waiting for transfers between devices, on_device(): key_part = lax.all_gather(key_rows, 'ep', axis=0, tiled=True)  34.1 us
    dot_general x6, matrix products, contract_rows(): lax.dot_general(left, right, (((0,), (0,)), ((), ())), preferred_element_...  30.2 us
    dot_general x4, matrix products, contract_cols(): lax.dot_general(left, right, (((1,), (1,)), ((), ())), preferred_element_...  29.9 us
  transfers between devices with their start and end apart: 9, of which 9 were waited for; matrix products, arithmetic and copies ran while one was open for 9% of the time, Pallas kernels for 0%

commit v1 on v0

v1 whole, which is shorter than its diff:
```python
import functools
import jax
import jax.numpy as jnp
from jax import lax
from jax.experimental import pallas as pl
from jax.experimental.pallas import tpu as pltpu
from jax.sharding import PartitionSpec as P

HEADS = 16
EPSILON = 1e-05
HEAD=64
BQ=256
MASKED=-1e30
F32=jnp.float32; BF=jnp.bfloat16
NT=(((1,),(1,)),((),()))
NN=(((1,),(0,)),((),()))
def dot(a,b,dims): return lax.dot_general(a,b,dims,preferred_element_type=F32)

def start_row(len_ref, first, width):
    pos = first + lax.broadcasted_iota(jnp.int32,(1,width),1)
    start = jnp.zeros((1,width),jnp.int32)
    edge = jnp.int32(0)
    for s in range(len_ref.shape[1]-1):
        edge = edge + len_ref[0,s]
        start = jnp.where(pos>=edge, edge, start)
    return pos, start

def split_heads(block, heads):
    if heads==1: return [block]
    lane = lax.broadcasted_iota(jnp.int32, block.shape, 1)
    return [jnp.where((lane>=h*HEAD)&(lane<(h+1)*HEAD), block, jnp.zeros_like(block)) for h in range(heads)]

def fwd_kernel(len_ref, q_ref, k_ref, v_ref, o_ref, lse_ref, vt_ref):
    rows, width = q_ref.shape
    heads = width//HEAD
    bk = BQ
    for b in range(rows//BQ):
        vt_ref[:, b*BQ:(b+1)*BQ] = v_ref[b*BQ:(b+1)*BQ,:].astype(F32).T.astype(BF)
    def qstep(i,_):
        base = pl.multiple_of(i*BQ,BQ)
        qb = q_ref[pl.ds(base,BQ),:]*BF(HEAD**-0.5)
        qh = split_heads(qb, heads)
        pos,start = start_row(len_ref, base, BQ)
        def kstep(j, carry, diag):
            kb = pl.multiple_of(j*bk,bk)
            kk = k_ref[pl.ds(kb,bk),:]
            key = kb + lax.broadcasted_iota(jnp.int32,(bk,BQ),0)
            ok = key>=start
            if diag: ok = ok & (key<=pos)
            out=[]
            for h in range(heads):
                m,l,acc = carry[h]
                s = jnp.where(ok, dot(kk,qh[h],NT), MASKED)
                nm = jnp.maximum(m, jnp.max(s,axis=0,keepdims=True))
                p = jnp.exp(s-nm)
                if diag: p = jnp.where(ok,p,0.0)
                al = jnp.exp(m-nm)
                l = l*al + jnp.sum(p,axis=0,keepdims=True)
                acc = acc*al + dot(vt_ref[h*HEAD:(h+1)*HEAD, pl.ds(kb,bk)], p.astype(BF), NN)
                out.append((nm,l,acc))
            return tuple(out)
        init = tuple((jnp.full((1,BQ),MASKED,F32),jnp.zeros((1,BQ),F32),jnp.zeros((HEAD,BQ),F32)) for _ in range(heads))
        c = kstep(i, init, True)
        c = lax.fori_loop(0,i,lambda j,c: kstep(j,c,False), c)
        o = jnp.concatenate([acc/l for m,l,acc in c],axis=0)
        o_ref[pl.ds(base,BQ),:] = o.T.astype(BF)
        lse_ref[:, pl.ds(base,BQ)] = jnp.concatenate([m+jnp.log(l) for m,l,acc in c]+[jnp.zeros((8-heads,BQ),F32)],axis=0)
        return 0
    lax.fori_loop(0, rows//BQ, qstep, 0)

def bwd_kernel(len_ref, q_ref, k_ref, v_ref, o_ref, g_ref, lse_ref, dq_ref, dk_ref, dv_ref, kt_ref, dka, dva):
    rows, width = q_ref.shape
    heads = width//HEAD
    bk = BQ
    dka[...] = jnp.zeros_like(dka); dva[...]=jnp.zeros_like(dva)
    for b in range(rows//BQ):
        kt_ref[:, b*BQ:(b+1)*BQ] = k_ref[b*BQ:(b+1)*BQ,:].astype(F32).T.astype(BF)
    def qstep(i,_):
        base = pl.multiple_of(i*BQ,BQ)
        qb = q_ref[pl.ds(base,BQ),:]*BF(HEAD**-0.5)
        gb = g_ref[pl.ds(base,BQ),:]
        qh = split_heads(qb, heads); gh = split_heads(gb, heads)
        go = (gb.astype(F32)*o_ref[pl.ds(base,BQ),:].astype(F32)).T
        deltas = [jnp.sum(go[h*HEAD:(h+1)*HEAD],axis=0,keepdims=True) for h in range(heads)]
        lses = [lse_ref[h:h+1, pl.ds(base,BQ)] for h in range(heads)]
        pos,start = start_row(len_ref, base, BQ)
        def kstep(j, dq, diag):
            kb = pl.multiple_of(j*bk,bk)
            kk = k_ref[pl.ds(kb,bk),:]; vv=v_ref[pl.ds(kb,bk),:]
            key = kb + lax.broadcasted_iota(jnp.int32,(bk,BQ),0)
            ok = key>=start
            if diag: ok = ok & (key<=pos)
            out=[]
            dk=dka[pl.ds(kb,bk),:]; dv=dva[pl.ds(kb,bk),:]
            for h in range(heads):
                s = dot(kk,qh[h],NT)
                p = jnp.where(ok, jnp.exp(s-lses[h]), 0.0)
                dp = dot(vv,gh[h],NT)
                ds = (p*(dp-deltas[h])).astype(BF)
                dv = dv + dot(p.astype(BF), gh[h], NN)
                dk = dk + dot(ds, qh[h], NN)
                out.append(dq[h] + dot(kt_ref[h*HEAD:(h+1)*HEAD, pl.ds(kb,bk)], ds, NN))
            dka[pl.ds(kb,bk),:]=dk; dva[pl.ds(kb,bk),:]=dv
            return tuple(out)
        dq = tuple(jnp.zeros((HEAD,BQ),F32) for _ in range(heads))
        dq = kstep(i,dq,True)
        dq = lax.fori_loop(0,i,lambda j,c:kstep(j,c,False),dq)
        dq_ref[pl.ds(base,BQ),:] = (jnp.concatenate(dq,axis=0).T*(HEAD**-0.5)).astype(BF)
        return 0
    lax.fori_loop(0, rows//BQ, qstep, 0)
    dk_ref[...] = dka[...].astype(BF); dv_ref[...]=dva[...].astype(BF)

VM=pl.BlockSpec(memory_space=pltpu.VMEM); SM=pl.BlockSpec(memory_space=pltpu.SMEM)
def attn_fwd(lengths,q,k,v):
    S,W=q.shape
    return pl.pallas_call(fwd_kernel,out_shape=(jax.ShapeDtypeStruct((S,W),BF),jax.ShapeDtypeStruct((8,S),F32)),
      in_specs=[SM,VM,VM,VM],out_specs=(VM,VM),scratch_shapes=[pltpu.VMEM((W,S),BF)],compiler_params=pltpu.CompilerParams(vmem_limit_bytes=40<<20))(lengths,q,k,v)
def attn_bwd(lengths,q,k,v,o,g,lse):
    S,W=q.shape
    sh=jax.ShapeDtypeStruct((S,W),BF)
    return pl.pallas_call(bwd_kernel,out_shape=(sh,sh,sh),
      in_specs=[SM]+[VM]*6,out_specs=(VM,VM,VM),scratch_shapes=[pltpu.VMEM((W,S),BF),pltpu.VMEM((S,W),F32),pltpu.VMEM((S,W),F32)],compiler_params=pltpu.CompilerParams(vmem_limit_bytes=40<<20))(lengths,q,k,v,o,g,lse)


def norm_forward(rows_in, gain_vec, shift_vec):
    average = jnp.mean(rows_in, axis=-1, keepdims=True)
    centered = rows_in - average
    inv_std = lax.rsqrt(jnp.mean(centered * centered, axis=-1, keepdims=True) + EPSILON)
    unit_rows = centered * inv_std
    return (unit_rows * gain_vec + shift_vec, unit_rows, inv_std)


def norm_backward(grad_rows, unit_rows, inv_std, gain_vec):
    grad_unit = grad_rows * gain_vec
    grad_in = inv_std * (
        grad_unit
        - jnp.mean(grad_unit, axis=-1, keepdims=True)
        - unit_rows * jnp.mean(grad_unit * unit_rows, axis=-1, keepdims=True)
    )
    return (grad_in, jnp.sum(grad_rows * unit_rows, axis=0), jnp.sum(grad_rows, axis=0))


def contract_rows(left, right):
    return lax.dot_general(
        left, right, (((0,), (0,)), ((), ())), preferred_element_type=jnp.float32
    )


def contract_cols(left, right):
    return lax.dot_general(
        left, right, (((1,), (1,)), ((), ())), preferred_element_type=jnp.float32
    )


def exchange(blocks):
    return lax.all_to_all(blocks, "ep", split_axis=0, concat_axis=0, tiled=True)


def on_device(
    tokens,
    gain_attn,
    shift_attn,
    w_qkv,
    w_o,
    gain_ffn,
    shift_ffn,
    w_in,
    w_out,
    seq_lengths,
    expert_ids,
    cotangent,
):
    rows, width = tokens.shape
    ranks = lax.axis_size("ep")
    copies = lax.axis_size("dp")
    own = width // ranks
    capacity = 2 * rows // ranks
    inputs = tokens.astype(jnp.float32)
    weight_in = w_in[0]
    weight_out = w_out[0]
    hidden = weight_in.shape[0]
    part = hidden // copies
    my_copy = lax.axis_index("dp")
    part_in = lax.dynamic_slice_in_dim(weight_in, my_copy * part, part, 0)
    part_out = lax.dynamic_slice_in_dim(weight_out, my_copy * part, part, 0)

    chosen_ids = expert_ids[:, 0]
    one_hot = (chosen_ids[:, None] == jnp.arange(ranks, dtype=jnp.int32)[None, :]).astype(jnp.int32)
    slot_of = jnp.sum((jnp.cumsum(one_hot, axis=0) - 1) * one_hot, axis=1)
    target = chosen_ids * capacity + slot_of
    placing = (
        jnp.arange(ranks * capacity, dtype=jnp.int32)[:, None] == target[None, :]
    ).astype(jnp.bfloat16)

    def dispatch(values):
        out = jnp.dot(placing, values, preferred_element_type=jnp.float32).astype(jnp.bfloat16)
        return exchange(out.reshape(ranks, capacity, width)).reshape(-1, width)

    g_own = dispatch(cotangent)
    g_all = lax.all_gather(g_own, "dp", axis=0, tiled=True)

    normed, unit_attn, inv_attn = norm_forward(inputs, gain_attn, shift_attn)
    normed_low = normed.astype(jnp.bfloat16)
    normed_all = lax.all_gather(normed_low, "ep", axis=0, tiled=True)
    qkv = jnp.dot(normed_low, w_qkv, preferred_element_type=jnp.float32).astype(jnp.bfloat16)
    to_heads = qkv.reshape(rows, 3, ranks, own).transpose(2, 0, 1, 3).reshape(ranks, rows, 3 * own)
    mine = exchange(to_heads).reshape(ranks * rows, 3 * own)
    queries, keys, values = mine[:, :own], mine[:, own : 2 * own], mine[:, 2 * own :]
    att_heads, lse = attn_fwd(seq_lengths, queries, keys, values)
    attended_low = (
        exchange(att_heads.reshape(ranks, rows, own)).transpose(1, 0, 2).reshape(rows, width)
    )
    hidden_res = inputs + jnp.dot(attended_low, w_o, preferred_element_type=jnp.float32)
    routed, unit_ffn, inv_ffn = norm_forward(hidden_res, gain_ffn, shift_ffn)
    routed_low = routed.astype(jnp.bfloat16)

    x_own = dispatch(routed_low)
    x_all = lax.all_gather(x_own, "dp", axis=0, tiled=True)
    pre = contract_cols(x_own, weight_in)
    grad_act = contract_cols(g_own, weight_out)
    act, gelu_pull = jax.vjp(lambda inner: jax.nn.gelu(inner, approximate=True), pre)
    grad_pre = gelu_pull(grad_act)[0].astype(jnp.bfloat16)
    grad_rows = jnp.dot(grad_pre, weight_in, preferred_element_type=jnp.float32).astype(
        jnp.bfloat16
    )
    grad_back = exchange(grad_rows.reshape(ranks, capacity, width))
    grad_routed = contract_rows(placing, grad_back.reshape(-1, width))
    produced = jnp.dot(
        act.astype(jnp.bfloat16), weight_out, preferred_element_type=jnp.float32
    ).astype(jnp.bfloat16)
    returned = exchange(produced.reshape(ranks, capacity, width))
    expert_rows = contract_rows(placing, returned.reshape(-1, width))
    block_out = (hidden_res + expert_rows).astype(jnp.bfloat16)

    grad_normed2, grad_gain_ffn, grad_shift_ffn = norm_backward(
        grad_routed, unit_ffn, inv_ffn, gain_ffn
    )
    grad_hidden = cotangent.astype(jnp.float32) + grad_normed2
    grad_hidden_low = grad_hidden.astype(jnp.bfloat16)
    grad_att = contract_cols(grad_hidden_low, w_o).astype(jnp.bfloat16)
    grad_att_heads = exchange(grad_att.reshape(rows, ranks, own).transpose(1, 0, 2)).reshape(
        ranks * rows, own
    )
    gh_all = lax.all_gather(grad_hidden_low, "ep", axis=0, tiled=True)
    dq, dk, dv = attn_bwd(seq_lengths, queries, keys, values, att_heads, grad_att_heads, lse)
    dqkv = jnp.concatenate([dq, dk, dv], axis=1)
    dqkv_back = exchange(dqkv.reshape(ranks, rows, 3 * own))
    grad_qkv = dqkv_back.reshape(ranks, rows, 3, own).transpose(1, 2, 0, 3).reshape(rows, 3 * width)
    grad_normed1 = contract_cols(grad_qkv, w_qkv)
    grad_in1, grad_gain_attn, grad_shift_attn = norm_backward(
        grad_normed1, unit_attn, inv_attn, gain_attn
    )
    grad_tokens = grad_hidden + grad_in1

    pre_part = contract_cols(x_all, part_in)
    act_part, part_pull = jax.vjp(lambda inner: jax.nn.gelu(inner, approximate=True), pre_part)
    grad_pre_part = part_pull(contract_cols(g_all, part_out))[0].astype(jnp.bfloat16)
    grad_w_in = contract_rows(grad_pre_part, x_all)[None]
    grad_w_out = contract_rows(act_part.astype(jnp.bfloat16), g_all)[None]

    g_w_qkv = contract_rows(normed_all, dqkv)
    g_w_o = contract_rows(gh_all, att_heads)
    both = jnp.concatenate([g_w_qkv, g_w_o], axis=1).astype(jnp.bfloat16)
    both = lax.psum_scatter(both, "dp", scatter_dimension=0, tiled=True)
    both = lax.all_gather(both, ("dp", "ep"), axis=0, tiled=True)
    both = both.reshape(copies, ranks, width // copies, 4, own).astype(jnp.float32)
    g_qkv_out = both[:, :, :, :3].transpose(0, 2, 3, 1, 4).reshape(width, 3 * width)
    g_o_out = both[:, :, :, 3].transpose(1, 3, 0, 2).reshape(width, width)
    summed = lax.psum(
        (grad_gain_attn, grad_shift_attn, grad_gain_ffn, grad_shift_ffn), ("dp", "ep")
    )
    return (
        block_out,
        grad_tokens,
        g_qkv_out,
        g_o_out,
        summed[0],
        summed[1],
        summed[2],
        summed[3],
        grad_w_in,
        grad_w_out,
    )


def solution(mesh):
    return jax.shard_map(
        on_device,
        mesh=mesh,
        in_specs=(
            P(("dp", "ep"), None),
            P(),
            P(),
            P(),
            P(),
            P(),
            P(),
            P("ep", None, None),
            P("ep", None, None),
            P("dp", None),
            P(("dp", "ep"), None),
            P(("dp", "ep"), None),
        ),
        out_specs=(
            P(("dp", "ep"), None),
            P(("dp", "ep"), None),
            P(),
            P(),
            P(),
            P(),
            P(),
            P(),
            P("ep", "dp", None),
            P("ep", "dp", None),
        ),
        check_vma=False,
    )
```

time: 1050 us -> 618 us (0.59)
  waiting for transfers between devices: 645 us -> 219 us
  matrix products: 201 us -> 118 us
  Pallas kernels: 0 us -> 51.9 us
  local copies, waits for them, and re-layouts: 65 us -> 86.3 us
  other arithmetic: 38.6 us -> 21.6 us
  starting transfers between devices: 14.3 us -> 26.4 us
  blocking collectives: 62 us -> 72.5 us
    psum x1 -> x0, waiting for transfers between devices: 269 us -> none  [on_device(): lax.psum((grad_w_qkv, grad_w_o, grad_gain_attn, grad_shift_attn, grad_gai...]
    reduce_scatter x3 -> x1, waiting for transfers between devices: 269 us -> 27.4 us  [on_device(): both = lax.psum_scatter(both, 'dp', scatter_dimension=0, tiled=True)]
    dot_general x10 -> x3, matrix products: 125 us -> 16.2 us  [the longest x1 12.2 us: on_device(): jnp.dot(act.astype(jnp.bfloat16), weight_out, preferred_element_type=jnp....]
    pallas_call x0 -> x2, Pallas kernels: none -> 51.9 us  [the longest x1 27.5 us: attn_fwd(): pl.pallas_call(fwd_kernel, out_shape=(jax.ShapeDtypeStruct((S, W), BF), j...]
    all_to_all x3 -> x6, waiting for transfers between devices: 31.7 us -> 83.5 us  [exchange(): return lax.all_to_all(blocks, 'ep', split_axis=0, concat_axis=0, tiled=True)]
    all_gather x2 -> x5, waiting for transfers between devices: 73.3 us -> 106 us  [the longest x1 58.4 us: on_device(): both = lax.all_gather(both, ('dp', 'ep'), axis=0, tiled=True)]
    transpose x0 -> x5, local copies, waits for them, and re-layouts: none -> 32.3 us  [the longest x2 24.7 us: on_device(): both[:, :, :, :3].transpose(0, 2, 3, 1, 4).reshape(width, 3 * width)]
    another operation x5 -> x1, local copies, waits for them, and re-layouts: 25.9 us -> 0.01 us
  transfers between devices with their start and end apart: 9 -> 12, of which waited for: 9 -> 9; matrix products, arithmetic and copies ran while one was open for 9% -> 21% of each run, Pallas kernels for 0% -> 9%
where the time goes in v1:
time: 618 us; the launch traced here: 610 us
  waiting for transfers between devices  219 us (35%)
  matrix products  118 us (19%)
  local copies, waits for them, and re-layouts  86.3 us (14%)
  blocking collectives  72.5 us (12%)
  Pallas kernels  51.9 us (8%)
  starting transfers between devices  26.4 us (4%)
  other arithmetic  21.6 us (3%)
  between operations  14.9 us (2%)
    all_to_all x6, waiting for transfers between devices, exchange(): return lax.all_to_all(blocks, 'ep', split_axis=0, concat_axis=0, tiled=True)  83.5 us
    all_gather x1, waiting for transfers between devices, on_device(): both = lax.all_gather(both, ('dp', 'ep'), axis=0, tiled=True)  58.4 us
    all_gather x1, waiting for transfers between devices, on_device(): g_all = lax.all_gather(g_own, 'dp', axis=0, tiled=True)  48 us
    dot_general x6, matrix products, contract_rows(): lax.dot_general(left, right, (((0,), (0,)), ((), ())), preferred_element_...  44 us
    psum x1, blocking collectives, on_device(): lax.psum((grad_gain_attn, grad_shift_attn, grad_gain_ffn, grad_shift_ffn)...  38.5 us
    all_to_all x2, blocking collectives, exchange(): return lax.all_to_all(blocks, 'ep', split_axis=0, concat_axis=0, tiled=True)  34 us
    dot_general x4, matrix products, contract_cols(): lax.dot_general(left, right, (((1,), (1,)), ((), ())), preferred_element_...  29.3 us
    pallas_call x1, Pallas kernels, attn_fwd(): pl.pallas_call(fwd_kernel, out_shape=(jax.ShapeDtypeStruct((S, W), BF), j...  27.5 us
  transfers between devices with their start and end apart: 12, of which 9 were waited for; matrix products, arithmetic and copies ran while one was open for 21% of the time, Pallas kernels for 9%

profile of v1, /device:TPU:0, one launch (start us, length us, event | category | flops | bytes accessed | tf_op | source)
XLA Modules:
  0.0 610.4 jit_solution(12773479630638591806)
XLA Ops:
  11.2 4.8 fusion.54
  20.3 5.2 all-to-all-start
  26.3 25.7 %all-to-all-done = bf16[8,256,384]{1,2,0:T(8,128)(2,1)} async-done(((bf16[8,256,384]{1,2,0:T(8,128)(2,1)}), bf16[8,256,384]{1,2,0:T(8,128)(2,1)}, u32[]{:S(2)}, u32[]{:S(2)}) %all-to-all-start) | async-done | bytes 1572896 | tf_op jit(solution)/shard_map/all_to_all | solution.py:156
  56.0 27.5 %shard_map.195 = (bf16[2048,128]{1,0:T(8,128)(2,1)S(1)}, f32[8,2048]{1,0:T(8,128)S(1)}) custom-call(s32[1,4]{1,0:T(1,128)S(1)} %copy-done.7, bf16[2048,128]{1,0:T(8,128)(2,1)S(1)} %get-tuple-element.36.q_ref, bf16[2048,128]{1,0:T(8,128)(2,1)S(1)} %get-tuple-element.35.k_ref, bf16[2048,128]{1,0:T(8,128)(2,1)S(1)} %get-tuple-element.34.v_ref), custom_call_target="tpu_custom_call" | custom-call | tf_op jit(solution)/shard_map/pallas_call | solution.py:116
  92.2 8.8 %all-to-all-done.1 = bf16[8,256,128]{1,2,0:T(8,128)(2,1)} async-done(((bf16[8,256,128]{1,2,0:T(8,128)(2,1)}), bf16[8,256,128]{1,2,0:T(8,128)(2,1)}, u32[]{:S(2)}, u32[]{:S(2)}) %all-to-all-start.1) | async-done | bytes 524320 | tf_op jit(solution)/shard_map/all_to_all | solution.py:156
  105.6 4.2 all-to-all-start.2
  112.3 13.0 %all-to-all-done.2 = bf16[8,64,1024]{2,1,0:T(8,128)(2,1)} async-done(((bf16[8,64,1024]{2,1,0:T(8,128)(2,1)}), bf16[8,64,1024]{2,1,0:T(8,128)(2,1)}, u32[]{:S(2)}, u32[]{:S(2)}) %all-to-all-start.2) | async-done | bytes 1048608 | tf_op jit(solution)/shard_map/all_to_all | solution.py:156
  125.3 4.3 all-to-all-start.4
  129.8 11.7 %fusion.20 = f32[512,4096]{1,0:T(8,128)} fusion(bf16[512,1024]{1,0:T(8,128)(2,1)} %bitcast.11, bf16[1,4096,1024]{2,1,0:T(8,128)(2,1)} %param.19), kind=kOutput, calls=%fused_computation.25 | convolution fusion | flops 4294967296 | bytes 17825792 | tf_op jit(solution)/shard_map/dot_general | solution.py:150
  145.0 21.3 %fusion.44 = bf16[512,1024]{1,0:T(8,128)(2,1)} fusion(bf16[1,4096,1024]{2,1,0:T(8,128)(2,1)} %param.19, f32[512,4096]{1,0:T(8,128)} %fusion.20, bf16[512,1024]{1,0:T(8,128)(2,1)} %bitcast.17, bf16[1,4096,1024]{2,1,0:T(8,128)(2,1)} %param.20), kind=kOutput, calls=%fused_computation.48 | convolution fusion | flops 8632401920 | bytes 27262976 | tf_op jit(solution)/shard_map/dot_general | solution.py:223
  166.3 18.8 %all_to_all.40 = bf16[8,64,1024]{2,1,0:T(8,128)(2,1)S(1)} all-to-all(bf16[8,64,1024]{2,1,0:T(8,128)(2,1)} %bitcast.134), channel_id=1, replica_groups=mesh['dp'=4,'ep'=8] {'ep'}, dimensions={0} | all-to-all | bytes 2097152 | tf_op jit(solution)/shard_map/all_to_all | solution.py:156
  192.1 15.2 %all_to_all.41 = bf16[8,256,128]{2,1,0:T(8,128)(2,1)S(1)} all-to-all(bf16[8,256,128]{2,1,0:T(8,128)(2,1)S(1)} %bitcast.130), channel_id=1, replica_groups=mesh['dp'=4,'ep'=8] {'ep'}, dimensions={0} | all-to-all | bytes 1048576 | tf_op jit(solution)/shard_map/all_to_all | solution.py:156
  209.3 24.4 %shard_map.196 = (bf16[2048,128]{1,0:T(8,128)(2,1)S(1)}, bf16[2048,128]{1,0:T(8,128)(2,1)S(1)}, bf16[2048,128]{1,0:T(8,128)(2,1)S(1)}) custom-call(s32[1,4]{1,0:T(1,128)S(1)} %copy-done.7, bf16[2048,128]{1,0:T(8,128)(2,1)S(1)} %copy-done.3, bf16[2048,128]{1,0:T(8,128)(2,1)S(1)} %get-tuple-element.35.k_ref, bf16[2048,128]{1,0:T(8,128)(2,1)S(1)} %get-tuple-element.34.v_ref, ...), custom_call_target="tpu_custom_call" | custom-call | tf_op jit(solution)/shard_map/pallas_call | solution.py:121
  236.3 4.5 convolution_convert_fusion.3
  246.1 27.4 %reduce-scatter.2.cloned.1.call-done = bf16[256,512]{0,1:T(8,128)(2,1)} async-done(((bf16[1024,512]{0,1:T(8,128)(2,1)}), bf16[256,512]{0,1:T(8,128)(2,1)}) %reduce-scatter.2.cloned.1.call-update) | async-done | bytes 262160 | tf_op jit(solution)/shard_map/reduce_scatter | solution.py:264
  273.5 12.2 %fusion.51 = bf16[512,1024]{1,0:T(8,128)(2,1)} fusion(bf16[1,4096,1024]{2,1,0:T(8,128)(2,1)} %param.20, f32[512,4096]{1,0:T(8,128)} %fusion.20), kind=kOutput, calls=%fused_computation.49 | convolution fusion | flops 4314365952 | bytes 17825792 | tf_op jit(solution)/shard_map/dot_general | solution.py:228
  292.0 12.8 %all-to-all-done.3 = bf16[8,64,1024]{2,1,0:T(8,128)(2,1)S(1)} async-done(((bf16[8,64,1024]{2,1,0:T(8,128)(2,1)}), bf16[8,64,1024]{2,1,0:T(8,128)(2,1)S(1)}, u32[]{:S(2)}, u32[]{:S(2)}) %all-to-all-start.3) | async-done | bytes 1048608 | tf_op jit(solution)/shard_map/all_to_all | solution.py:156
  304.8 4.3 all-to-all-start.7
  310.4 19.7 %all-to-all-done.7 = bf16[8,256,384]{1,2,0:T(8,128)(2,1)} async-done(((bf16[8,256,384]{1,2,0:T(8,128)(2,1)}), bf16[8,256,384]{1,2,0:T(8,128)(2,1)}, u32[]{:S(2)}, u32[]{:S(2)}) %all-to-all-start.7) | async-done | bytes 1572896 | tf_op jit(solution)/shard_map/all_to_all | solution.py:156
  331.7 5.1 fusion.69
  336.8 38.5 %all-reduce = (f32[1024]{0:T(1024)}, f32[1024]{0:T(1024)}, f32[1024]{0:T(1024)}, f32[1024]{0:T(1024)}) all-reduce(f32[1024]{0:T(1024)S(1)} %get-tuple-element.22, f32[1024]{0:T(1024)S(1)} %get-tuple-element.27, f32[1024]{0:T(1024)S(1)} %get-tuple-element.20, f32[1024]{0:T(1024)S(1)} %get-tuple-element.26), channel_id=1, replica_groups=mesh['dp'=4,'ep'=8] {'dp','ep'}, use_global_device_ids=true, to_apply=%region_13.14 | all-reduce | flops 4096 | bytes 32768 | tf_op jit(solution)/shard_map/psum | solution.py:269
  376.7 10.8 %fusion.38 = f32[2048,1024]{1,0:T(8,128)} fusion(bf16[2048,1024]{1,0:T(8,128)(2,1)} %all-gather.14.cloned.1.call-done, bf16[1,4096,1024]{2,1,0:T(8,128)(2,1)} %param.19, s32[]{:T(128)S(6)} %select_n.4), kind=kOutput, calls=%fused_computation.39 | convolution fusion | flops 4294967296 | bytes 14680068 | tf_op jit(solution)/shard_map/dot_general | solution.py:150
  387.5 48.0 %all-gather.12.cloned.1.call-done = bf16[2048,1024]{1,0:T(8,128)(2,1)} async-done(((bf16[512,1024]{1,0:T(8,128)(2,1)}), bf16[2048,1024]{1,0:T(8,128)(2,1)}) %all-gather.12.cloned.1.call-update) | async-done | bytes 4194320 | tf_op jit(solution)/shard_map/all_gather | solution.py:200
  435.5 12.1 %fusion.37 = f32[1,1024,1024]{2,1,0:T(8,128)} fusion(bf16[2048,1024]{1,0:T(8,128)(2,1)} %all-gather.12.cloned.1.call-done, f32[2048,1024]{1,0:T(8,128)} %fusion.38), kind=kOutput, calls=%fused_computation.38 | convolution fusion | flops 4313841664 | bytes 16777216 | tf_op jit(solution)/shard_map/dot_general | solution.py:144
  447.5 21.2 %fusion.34 = f32[1,1024,1024]{2,1,0:T(8,128)} fusion(bf16[2048,1024]{1,0:T(8,128)(2,1)} %all-gather.14.cloned.1.call-done, f32[2048,1024]{1,0:T(8,128)} %fusion.38, bf16[2048,1024]{1,0:T(8,128)(2,1)} %all-gather.12.cloned.1.call-done, bf16[1,4096,1024]{2,1,0:T(8,128)(2,1)} %param.20, s32[]{:T(128)S(6)} %select_n.4), kind=kOutput, calls=%fused_computation.37 | convolution fusion | flops 8631877632 | bytes 23068676 | tf_op jit(solution)/shard_map/dot_general | solution.py:144
  468.7 58.4 %all-gather.10.cloned.1.call-done = bf16[8192,512]{0,1:T(8,128)(2,1)} async-done(((bf16[256,512]{0,1:T(8,128)(2,1)}), bf16[8192,512]{0,1:T(8,128)(2,1)}) %all-gather.10.cloned.1.call-update) | async-done | bytes 8388624 | tf_op jit(solution)/shard_map/all_gather | solution.py:265
  527.1 11.3 %convert_element_type.80 = f32[8192,512]{0,1:T(8,128)} convert(bf16[8192,512]{0,1:T(8,128)(2,1)} %all-gather.10.cloned.1.call-done) | non-fusion elementwise | flops 4194304 | bytes 25165824 | tf_op jit(solution)/shard_map/convert_element_type | solution.py:266
  538.5 11.1 %copy.36 = f32[64,8,32,256]{3,2,1,0:T(8,128)S(1)} copy(f32[64,8,32,256]{3,1,2,0:T(8,128)} %bitcast.121) | data formatting | bytes 33554432
  549.6 5.7 copy-done.8
  557.6 12.1 %slice_bitcast_fusion = f32[4,256,3,8,128]{1,3,0,4,2:T(8,128)} fusion(f32[4,8,256,4,128]{2,1,0,4,3:T(8,128)} %bitcast.120), kind=kLoop, calls=%fused_computation | loop fusion | bytes 25165824 | tf_op jit(solution)/shard_map/transpose | solution.py:267
  569.7 12.6 %copy.32 = f32[4,256,3,8,128]{4,3,2,1,0:T(8,128)} copy(f32[4,256,3,8,128]{1,3,0,4,2:T(8,128)} %slice_bitcast_fusion) | data formatting | bytes 25165824 | tf_op jit(solution)/shard_map/transpose | solution.py:267
  582.3 13.9 %reshape.174 = f32[1024,3072]{1,0:T(8,128)} reshape(f32[4,256,3,8,128]{4,3,2,1,0:T(8,128)} %copy.32) | data formatting | bytes 25165824 | tf_op jit(solution)/shard_map/reshape | solution.py:267
  (95 shorter events, 69.0 us)
Async XLA Ops:
  7.2 93.9 %copy-start = (bf16[1024,1024]{1,0:T(8,128)(2,1)S(1)}, bf16[1024,1024]{1,0:T(8,128)(2,1)}, u32[]{:S(2)}) copy-start(bf16[1024,1024]{1,0:T(8,128)(2,1)} %param.16) | copy-start | bytes 6291460
  11.2 4.8 copy-start.13
  16.0 39.9 %copy-start.7 = (s32[1,4]{1,0:T(1,128)S(1)}, s32[1,4]{1,0:T(1,128)}, u32[]{:S(2)}) copy-start(s32[1,4]{1,0:T(1,128)} %len_ref.3) | copy-start | bytes 52
  17.5 73.8 %copy-start.16 = (s32[256,1]{0,1:T(1,128)S(1)}, s32[256,1]{0,1:T(1,128)}, u32[]{:S(2)}) copy-start(s32[256,1]{0,1:T(1,128)} %param.22) | copy-start | bytes 3076
  20.3 31.6 %all-to-all-start = ((bf16[8,256,384]{1,2,0:T(8,128)(2,1)}), bf16[8,256,384]{1,2,0:T(8,128)(2,1)}, u32[]{:S(2)}, u32[]{:S(2)}) async-start(bf16[8,256,384]{1,2,0:T(8,128)(2,1)} %bitcast.123), calls=%async_computation | async-start | bytes 3145728 | tf_op jit(solution)/shard_map/all_to_all | solution.py:156
  25.5 78.5 %copy-start.15 = (f32[1024]{0:T(1024)S(1)}, f32[1024]{0:T(1024)}, u32[]{:S(2)}) copy-start(f32[1024]{0:T(1024)} %param.17) | copy-start | bytes 12292
  25.5 78.5 %copy-start.17 = (f32[1024]{0:T(1024)S(1)}, f32[1024]{0:T(1024)}, u32[]{:S(2)}) copy-start(f32[1024]{0:T(1024)} %param.18) | copy-start | bytes 12292
  25.5 210.7 %all-gather.6.cloned.1.call-start = ((), (), s32[]{:S(2)}) async-start(), calls=%async_computation.9 | async-start | bytes 4718592 | tf_op jit(solution)/shard_map/all_gather | solution.py:204
  83.5 0.8 copy-start.2
  84.3 0.8 copy-start.4
  87.1 13.9 %all-to-all-start.1 = ((bf16[8,256,128]{1,2,0:T(8,128)(2,1)}), bf16[8,256,128]{1,2,0:T(8,128)(2,1)}, u32[]{:S(2)}, u32[]{:S(2)}) async-start(bf16[8,256,128]{1,2,0:T(8,128)(2,1)} %copy.28), calls=%async_computation.1 | async-start | bytes 1048576 | tf_op jit(solution)/shard_map/all_to_all | solution.py:156
  103.0 1.0 copy-start.9
  105.6 19.7 %all-to-all-start.2 = ((bf16[8,64,1024]{2,1,0:T(8,128)(2,1)}), bf16[8,64,1024]{2,1,0:T(8,128)(2,1)}, u32[]{:S(2)}, u32[]{:S(2)}) async-start(bf16[8,64,1024]{2,1,0:T(8,128)(2,1)} %bitcast.129), calls=%async_computation.2 | async-start | bytes 2097152 | tf_op jit(solution)/shard_map/all_to_all | solution.py:156
  125.3 19.7 %all-to-all-start.4 = ((bf16[8,64,1024]{2,1,0:T(8,128)(2,1)}), bf16[8,64,1024]{2,1,0:T(8,128)(2,1)}, u32[]{:S(2)}, u32[]{:S(2)}) async-start(bf16[8,64,1024]{2,1,0:T(8,128)(2,1)} %bitcast.128), calls=%async_computation.4 | async-start | bytes 2097152 | tf_op jit(solution)/shard_map/all_to_all | solution.py:156
  129.6 111.2 %all-gather.8.cloned.1.call-start = ((), (), s32[]{:S(2)}) async-start(), calls=%async_computation.10 | async-start | bytes 4718592 | tf_op jit(solution)/shard_map/all_gather | solution.py:244
  190.1 83.3 %reduce-scatter.2.cloned.1.call-start = ((), (), s32[]{:S(2)}) async-start(), calls=%async_computation.11 | async-start | bytes 1310720 | tf_op jit(solution)/shard_map/reduce_scatter | solution.py:264
  207.2 1.0 copy-start.3
  208.3 1.0 copy-start.5
  233.8 7.0 %copy-start.6 = (bf16[2048,128]{1,0:T(8,128)(2,1)S(1)}, bf16[2048,128]{1,0:T(8,128)(2,1)}, u32[]{:S(2)}) copy-start(bf16[2048,128]{1,0:T(8,128)(2,1)} %copy-done.4) | copy-start | bytes 1572868
  244.8 131.8 %all-gather.14.cloned.1.call-start = ((), (), s32[]{:S(2)}) async-start(), calls=%async_computation.14 | async-start | bytes 5242880 | tf_op jit(solution)/shard_map/all_gather | solution.py:218
  245.4 190.0 %all-gather.12.cloned.1.call-start = ((), (), s32[]{:S(2)}) async-start(), calls=%async_computation.13 | async-start | bytes 5242880 | tf_op jit(solution)/shard_map/all_gather | solution.py:200
  246.0 281.1 %all-gather.10.cloned.1.call-start = ((), (), s32[]{:S(2)}) async-start(), calls=%async_computation.12 | async-start | bytes 8650752 | tf_op jit(solution)/shard_map/all_gather | solution.py:265
  285.6 23.5 %copy-start.10 = (f32[256,1024]{1,0:T(8,128)S(1)}, f32[256,1024]{1,0:T(8,128)}, u32[]{:S(2)}) copy-start(f32[256,1024]{1,0:T(8,128)} %copy-done.9) | copy-start | bytes 3145732
  285.6 46.1 %copy-start.11 = (bf16[256,1024]{1,0:T(8,128)(2,1)S(1)}, bf16[256,1024]{1,0:T(8,128)(2,1)}, u32[]{:S(2)}) copy-start(bf16[256,1024]{1,0:T(8,128)(2,1)} %param.12) | copy-start | bytes 1572868
  285.6 46.1 %copy-start.14 = (f32[1024]{0:T(1024)S(1)}, f32[1024]{0:T(1024)}, u32[]{:S(2)}) copy-start(f32[1024]{0:T(1024)} %param.13) | copy-start | bytes 12292
  285.6 19.2 %all-to-all-start.3 = ((bf16[8,64,1024]{2,1,0:T(8,128)(2,1)}), bf16[8,64,1024]{2,1,0:T(8,128)(2,1)S(1)}, u32[]{:S(2)}, u32[]{:S(2)}) async-start(bf16[8,64,1024]{2,1,0:T(8,128)(2,1)} %bitcast.132), calls=%async_computation.3 | async-start | bytes 2097152 | tf_op jit(solution)/shard_map/all_to_all | solution.py:156
  304.8 25.3 %all-to-all-start.7 = ((bf16[8,256,384]{1,2,0:T(8,128)(2,1)}), bf16[8,256,384]{1,2,0:T(8,128)(2,1)}, u32[]{:S(2)}, u32[]{:S(2)}) async-start(bf16[8,256,384]{1,2,0:T(8,128)(2,1)} %copy.30), calls=%async_computation.7 | async-start | bytes 3145728 | tf_op jit(solution)/shard_map/all_to_all | solution.py:156
  310.4 64.9 %copy-start.12 = (f32[256,1024]{1,0:T(8,128)S(1)}, f32[256,1024]{1,0:T(8,128)}, u32[]{:S(2)}) copy-start(f32[256,1024]{1,0:T(8,128)} %get-tuple-element.33) | copy-start | bytes 3145732
  549.6 5.7 copy-start.8
  582.3 20.8 %copy-start.1 = (bf16[1024,1024]{1,0:T(8,128)(2,1)S(1)}, bf16[1024,1024]{1,0:T(8,128)(2,1)}, u32[]{:S(2)}) copy-start(bf16[1024,1024]{1,0:T(8,128)(2,1)} %param.16) | copy-start | bytes 6291460
Sparse Core Ops, SparseCore 0:
  28.3 44.2 all-gather.5
  190.3 40.3 all-gather.7
  245.0 28.4 reduce-scatter.1
  274.9 79.5 all-gather.13
  356.0 79.3 all-gather.11
  438.6 88.4 all-gather.9

commit v2 on v1

v2 whole, which is shorter than its diff:
```python
import functools
import types

import jax
import jax.numpy as jnp
from jax import lax
from jax.experimental import pallas as pl
from jax.experimental.pallas import tpu as pltpu
from jax.sharding import PartitionSpec as P

HEADS = 16
EPSILON = 1e-05
MASKED = -1e30
TILE = 512
SMALL = 8
MESH = pl.DeviceIdType.MESH
F32 = jnp.float32
BF = jnp.bfloat16
NN = (((1,), (0,)), ((), ()))
NT = (((1,), (1,)), ((), ()))
TN = (((0,), (0,)), ((), ()))


def dot(left, right, dims):
    return lax.dot_general(left, right, dims, preferred_element_type=F32)


def partner(me, k, n):
    out, weight = 0, 1
    while weight < n:
        bit = lax.rem(lax.div(me, weight), 2)
        out = out + (lax.rem(bit + 1, 2) if k & weight else bit) * weight
        weight *= 2
    return out


def send(src, dst, send_sem, recv_sem, target):
    return pltpu.make_async_remote_copy(
        src_ref=src,
        dst_ref=dst,
        send_sem=send_sem,
        recv_sem=recv_sem,
        device_id=target,
        device_id_type=MESH,
    )


def order_of(n):
    return sorted(range(1, n), key=lambda k: (-bin(k // 2).count("1"), k))


def flat(value):
    return value.reshape(value.shape[0] * value.shape[1], value.shape[2])


def tiles(count, body):
    def step(t, _):
        body(pl.ds(pl.multiple_of(t * TILE, TILE), TILE))
        return 0

    lax.fori_loop(0, count // TILE, step, 0)


def norm_rows(rows_in):
    average = jnp.mean(rows_in, axis=-1, keepdims=True)
    centered = rows_in - average
    inv_std = lax.rsqrt(jnp.mean(centered * centered, axis=-1, keepdims=True) + EPSILON)
    return centered * inv_std, inv_std


CHUNK = 32


def by_rows(count, body, carry=0):
    def step(i, state):
        return body(pl.ds(pl.multiple_of(i * CHUNK, CHUNK), CHUNK), state)

    return lax.fori_loop(0, count // CHUNK, step, carry)


def norm_apply(src, gain, shift, dst):
    def body(at, _):
        unit, _ = norm_rows(src[at, :].astype(F32))
        dst[at, :] = (unit * gain[...] + shift[...]).astype(BF)
        return 0

    by_rows(src.shape[0], body)


def norm_back(src, grad, gain, store):
    def body(at, sums):
        unit, inv = norm_rows(src[at, :].astype(F32))
        incoming = grad[at, :]
        grad_unit = incoming * gain[...]
        grad_in = inv * (
            grad_unit
            - jnp.mean(grad_unit, axis=-1, keepdims=True)
            - unit * jnp.mean(grad_unit * unit, axis=-1, keepdims=True)
        )
        store(at, grad_in)
        return (
            sums[0] + jnp.sum(incoming * unit, axis=0, keepdims=True),
            sums[1] + jnp.sum(incoming, axis=0, keepdims=True),
        )

    zero = jnp.zeros((1, src.shape[1]), F32)
    return by_rows(src.shape[0], body, (zero, zero))


def gelu_both(pre):
    square = pre * pre
    bent = jnp.tanh(0.7978845608028654 * pre * (1.0 + 0.044715 * square))
    half = 0.5 + 0.5 * bent
    rise = 0.7978845608028654 * (1.0 + 3 * 0.044715 * square)
    return pre * half, half + 0.5 * pre * (1.0 - bent * bent) * rise


def place_matrix(ids_row, n, cap):
    rows = ids_row.shape[1]
    expert = lax.broadcasted_iota(jnp.int32, (n, rows), 0)
    hit = (expert == ids_row).astype(F32)
    before = lax.broadcasted_iota(jnp.int32, (rows, rows), 0)
    after = lax.broadcasted_iota(jnp.int32, (rows, rows), 1)
    upto = (before <= after).astype(F32).astype(BF)
    count = dot(hit.astype(BF), upto, NN)
    slot = jnp.sum(hit * (count - 1.0), axis=0, keepdims=True)
    target = ids_row * cap + slot.astype(jnp.int32)
    places = lax.broadcasted_iota(jnp.int32, (n * cap, rows), 0)
    return (places == target).astype(F32).astype(BF)


def start_row(len_ref, first, width):
    pos = first + lax.broadcasted_iota(jnp.int32, (1, width), 1)
    start = jnp.zeros((1, width), jnp.int32)
    edge = jnp.int32(0)
    for s in range(len_ref.shape[1] - 1):
        edge = edge + len_ref[0, s]
        start = jnp.where(pos >= edge, edge, start)
    return pos, start


def split_heads(block, heads):
    if heads == 1:
        return [block]
    size = block.shape[1] // heads
    lane = lax.broadcasted_iota(jnp.int32, block.shape, 1)
    zero = jnp.zeros_like(block)
    return [
        jnp.where((lane >= h * size) & (lane < (h + 1) * size), block, zero) for h in range(heads)
    ]


def attend_block(r, i):
    rows, own = r.qkv_heads.shape[2:]
    heads = r.heads
    size = own // heads
    queries = split_heads(r.qkv_heads[0, i] * BF(size**-0.5), heads)
    pos, start = start_row(r.lengths, i * rows, rows)

    def fold(j, carry, diagonal):
        keys = r.qkv_heads[1, j]
        key = j * rows + lax.broadcasted_iota(jnp.int32, (rows, rows), 0)
        allowed = key >= start
        if diagonal:
            allowed = allowed & (key <= pos)
        out = []
        for h in range(heads):
            top, total, accum = carry[h]
            scores = jnp.where(allowed, dot(keys, queries[h], NT), MASKED)
            new_top = jnp.maximum(top, jnp.max(scores, axis=0, keepdims=True))
            weights = jnp.exp(scores - new_top)
            if diagonal:
                weights = jnp.where(allowed, weights, 0.0)
            decay = jnp.exp(top - new_top)
            total = total * decay + jnp.sum(weights, axis=0, keepdims=True)
            values = r.values_t[j, h * size : (h + 1) * size, :]
            accum = accum * decay + dot(values, weights.astype(BF), NN)
            out.append((new_top, total, accum))
        return tuple(out)

    state = tuple(
        (
            jnp.full((1, rows), MASKED, F32),
            jnp.zeros((1, rows), F32),
            jnp.zeros((size, rows), F32),
        )
        for _ in range(heads)
    )
    state = fold(i, state, True)
    state = lax.fori_loop(0, i, lambda j, carry: fold(j, carry, False), state)
    result = jnp.concatenate([accum / total for _, total, accum in state], axis=0)
    r.att_heads[i] = result.T.astype(BF)
    sums = [top + jnp.log(total) for top, total, _ in state]
    r.lse[i] = jnp.concatenate(sums + [jnp.zeros((SMALL - heads, rows), F32)], axis=0)


def attend_back(r, j, n):
    rows, own = r.qkv_heads.shape[2:]
    heads = r.heads
    size = own // heads
    keys, values = r.qkv_heads[1, j], r.qkv_heads[2, j]
    keys_t = keys.astype(F32).T.astype(BF)

    def fold(i, carry, diagonal):
        grad_k, grad_v = carry
        queries = split_heads(r.qkv_heads[0, i] * BF(size**-0.5), heads)
        grads = split_heads(r.grad_att[i], heads)
        pos, start = start_row(r.lengths, i * rows, rows)
        key = j * rows + lax.broadcasted_iota(jnp.int32, (rows, rows), 0)
        allowed = key >= start
        if diagonal:
            allowed = allowed & (key <= pos)
        for h in range(heads):
            scores = dot(keys, queries[h], NT)
            probs = jnp.where(allowed, jnp.exp(scores - r.lse[i, h : h + 1, :]), 0.0)
            grad_probs = dot(values, grads[h], NT)
            grad_scores = (probs * (grad_probs - r.delta[i, h : h + 1, :])).astype(BF)
            grad_v = grad_v + dot(probs.astype(BF), grads[h], NN)
            grad_k = grad_k + dot(grad_scores, queries[h], NN)
            part = slice(h * size, (h + 1) * size)
            r.grad_q_t[i, part, :] += dot(keys_t[part, :], grad_scores, NN)
        return grad_k, grad_v

    zero = jnp.zeros((rows, own), F32)
    carry = fold(j, (zero, zero), True)
    grad_k, grad_v = lax.fori_loop(
        j + 1, n, lambda i, carry: fold(i, carry, False), carry
    )
    r.qkv_send[1, j] = grad_k.astype(BF)
    r.qkv_send[2, j] = grad_v.astype(BF)


class Chain:
    def __init__(self, block, whole, send_sem, recv_sem, at, c):
        self.block, self.whole, self.at, self.c = block, whole, at, c
        self.send_sem, self.recv_sem = send_sem, recv_sem

    def copy(self, way, stage):
        held = self.at - stage if way == 0 else self.at + stage
        target = self.at + 1 if way == 0 else self.at - 1
        src = self.block if stage == 0 else self.whole.at[held]
        return send(
            src,
            self.whole.at[held],
            self.send_sem.at[way, stage],
            self.recv_sem.at[way, stage],
            {"dp": target},
        )

    def sends(self, way, stage):
        if way == 0:
            return (self.at >= stage) & (self.at + 1 < self.c)
        return (self.at + stage < self.c) & (self.at >= 1)

    def gets(self, way, stage):
        return self.at >= stage + 1 if way == 0 else self.at + stage + 1 < self.c

    def start(self, stage):
        for way in range(2):
            if stage:

                @pl.when(self.gets(way, stage - 1))
                def _():
                    self.copy(way, stage - 1).wait_recv()

            @pl.when(self.sends(way, stage))
            def _():
                self.copy(way, stage).start()

    def finish(self):
        for way in range(2):

            @pl.when(self.gets(way, self.c - 2))
            def _():
                self.copy(way, self.c - 2).wait_recv()

            for stage in range(self.c - 1):

                @pl.when(self.sends(way, stage))
                def _():
                    self.copy(way, stage).wait_send()


class Spread:
    def __init__(self, r, name, me, grp, n, c, place):
        self.send_buf, self.recv_buf, self.final = (
            getattr(r, name + part) for part in ("_send", "_recv", "_fin")
        )
        self.ss, self.rs = getattr(r, name + "_ss"), getattr(r, name + "_rs")
        self.ys, self.yr = getattr(r, name + "_ys"), getattr(r, name + "_yr")
        self.me, self.grp, self.n, self.c, self.place = me, grp, n, c, place
        self.local = r.load_sem.at[getattr(r, name + "_slot")]
        self.direct = [k for k in order_of(n) if k % 2 == 0]

    def to_piece(self, t):
        target = lax.rem(self.grp + t, self.c)
        return send(
            self.send_buf.at[target],
            self.recv_buf.at[self.grp],
            self.ss.at[0, t],
            self.rs.at[0, t],
            {"dp": target},
        )

    def to_copies(self, t):
        return send(
            self.final,
            self.place(self.me, self.grp),
            self.ss.at[1, t],
            self.rs.at[1, t],
            {"dp": lax.rem(self.grp + t, self.c)},
        )

    def across(self, k):
        block = self.place(self.me, None)
        return send(
            block, block, self.ys.at[k], self.yr.at[k], {"ep": partner(self.me, k, self.n)}
        )

    def pass_on(self, k):
        block = self.place(partner(self.me, k, self.n), None)
        return send(
            block,
            block,
            self.ys.at[k + 1],
            self.yr.at[k + 1],
            {"ep": partner(self.me, 1, self.n)},
        )

    def scatter(self):
        for t in range(1, self.c):
            self.to_piece(t).start()
        self.recv_buf[self.grp] = self.send_buf[self.grp]

    def total(self):
        for t in range(1, self.c):
            self.to_piece(t).wait_recv()
        total = self.recv_buf[0].astype(F32)
        for s in range(1, self.c):
            total = total + self.recv_buf[s].astype(F32)
        self.final[...] = total.astype(BF)
        for t in range(1, self.c):
            self.to_copies(t).start()
        self.mine = pltpu.make_async_copy(
            self.final, self.place(self.me, self.grp), self.local
        )
        self.mine.start()

    def over(self):
        for t in range(1, self.c):
            self.to_copies(t).wait_recv()
        self.mine.wait()
        for k in self.direct + [1]:
            self.across(k).start()

    def share(self):
        for k in self.direct:
            self.across(k).wait_recv()
            self.pass_on(k).start()

    def finish(self):
        self.across(1).wait()
        for k in self.direct:
            self.across(k).wait_send()
            self.pass_on(k).wait()
        for t in range(1, self.c):
            self.to_piece(t).wait_send()
            self.to_copies(t).wait_send()


def block_kernel(r, n, c):
    me, grp = lax.axis_index("ep"), lax.axis_index("dp")
    rows, width = r.tokens.shape
    own, cap = width // n, 2 * rows // n
    slots = n * cap
    hidden = r.w_in.shape[1]
    part = hidden // c
    order = order_of(n)
    direct = [k for k in order if k % 2 == 0]
    partners = {k: partner(me, k, n) for k in order}
    half = width // 2

    def to_partner(src, dst, send_sem, recv_sem, k):
        return send(src, dst, send_sem, recv_sem, {"ep": partners[k]})

    def blocks_out(buf, dst, sems, k):
        return to_partner(buf.at[partners[k]], dst.at[me], sems[0].at[k], sems[1].at[k], k)

    barrier = pltpu.get_barrier_semaphore()
    for k in order:
        pl.semaphore_signal(barrier, inc=1, device_id={"ep": partners[k]}, device_id_type=MESH)
    for t in range(1, c):
        pl.semaphore_signal(
            barrier, inc=1, device_id={"dp": lax.rem(grp + t, c)}, device_id_type=MESH
        )

    def load_qkv(slot):
        cols = pl.ds(0, 3 * width)
        return [
            pltpu.make_async_copy(
                r.w_qkv.at[pl.ds(0, half), :], r.act.at[:, cols], r.load_sem.at[slot]
            ),
            pltpu.make_async_copy(
                r.w_qkv.at[pl.ds(half, half), :], r.grad_pre.at[:, cols], r.load_sem.at[slot + 1]
            ),
        ]

    first_loads = load_qkv(0)
    load_o = pltpu.make_async_copy(r.w_o, r.w_o_v, r.load_sem.at[2])
    load_out = pltpu.make_async_copy(r.w_out.at[0], r.w_out_v, r.load_sem.at[3])
    load_in = pltpu.make_async_copy(r.w_in.at[0], r.w_in_v, r.load_sem.at[4])
    for load in first_loads + [load_o, load_out, load_in]:
        load.start()

    norm_apply(r.tokens, r.gain_attn, r.shift_attn, r.normed)
    pl.semaphore_wait(barrier, n - 1 + c - 1)

    def to_heads(p, k):
        return to_partner(
            r.qkv_send.at[p, partners[k]],
            r.qkv_heads.at[p, me],
            r.a_ss.at[p, k],
            r.a_rs.at[p, k],
            k,
        )

    for load in first_loads:
        load.wait()
    for p in range(3):
        for t in range(width // TILE):
            cols = slice(p * width + t * TILE, p * width + (t + 1) * TILE)
            block = dot(r.normed[:, :half], r.act[:, cols], NN)
            block = (block + dot(r.normed[:, half:], r.grad_pre[:, cols], NN)).astype(BF)
            for e in range(TILE // own):
                r.qkv_send[p, t * (TILE // own) + e] = block[:, e * own : (e + 1) * own]
        for k in order:
            to_heads(p, k).start()
        r.qkv_heads[p, me] = r.qkv_send[p, me]

    r.place[...] = place_matrix(r.ids[...], n, cap)
    for t in range(width // TILE):
        cols = slice(t * TILE, (t + 1) * TILE)
        r.g_send[:, :, cols] = (
            dot(r.place[...], r.cotangent[:, cols], NN).astype(BF).reshape(n, cap, TILE)
        )
    for p in range(3):
        for k in order:
            to_heads(p, k).wait_recv()
    g_copies = [blocks_out(r.g_send, r.g_own, (r.g_ss, r.g_rs), k) for k in order]
    for copy in g_copies:
        copy.start()
    r.g_own[me] = r.g_send[me]

    def gather(k):
        return to_partner(r.normed, r.normed_all.at[me], r.n_ss.at[k], r.n_rs.at[k], k)

    def pass_on(k):
        src = r.normed_all.at[partners[k]]
        return to_partner(src, src, r.n_ss.at[k + 1], r.n_rs.at[k + 1], 1)

    for k in direct + [1]:
        gather(k).start()
    mine = pltpu.make_async_copy(r.normed, r.normed_all.at[me], r.load_sem.at[5])
    mine.start()

    for i in range(n):
        r.values_t[i] = r.qkv_heads[2, i].astype(F32).T.astype(BF)

    def home(t):
        target = lax.rem(me + t, n)
        return send(
            r.att_heads.at[target],
            r.att_recv.at[me],
            r.o_ss.at[t],
            r.o_rs.at[t],
            {"ep": target},
        )

    attend_block(r, me)
    r.att_recv[me] = r.att_heads[me]

    def block_step(t, _):
        attend_block(r, lax.rem(me + t, n))
        home(t).start()
        return 0

    lax.fori_loop(1, n // 2, block_step, 0)
    for copy in g_copies:
        copy.wait()
    g_chain = Chain(r.g_own, r.g_all, r.gz_ss, r.gz_rs, grp, c)
    x_chain = Chain(r.x_own, r.x_all, r.xz_ss, r.xz_rs, grp, c)
    g_chain.start(0)
    lax.fori_loop(n // 2, n, block_step, 0)
    for k in direct:
        gather(k).wait_recv()
        pass_on(k).start()
    for t in range(1, n):
        home(t).wait_recv()
    for e in range(n):
        r.attended[:, e * own : (e + 1) * own] = r.att_recv[e]

    load_o.wait()
    for t in range(width // TILE):
        cols = slice(t * TILE, (t + 1) * TILE)
        r.hidden[:, cols] = r.tokens[:, cols].astype(F32) + dot(
            r.attended[...], r.w_o_v[:, cols], NN
        )
    norm_apply(r.hidden, r.gain_ffn, r.shift_ffn, r.block_out)
    for t in range(width // TILE):
        cols = slice(t * TILE, (t + 1) * TILE)
        r.x_send[:, :, cols] = (
            dot(r.place[...], r.block_out[:, cols], NN).astype(BF).reshape(n, cap, TILE)
        )
    x_copies = [blocks_out(r.x_send, r.x_own, (r.x_ss, r.x_rs), k) for k in order]
    for copy in x_copies:
        copy.start()
    r.x_own[me] = r.x_send[me]
    g_chain.start(1)

    load_out.wait()

    def act_grad(t, _):
        at = pl.multiple_of(t * TILE, TILE)
        r.grad_pre[:, pl.ds(at, TILE)] = dot(
            flat(r.g_own[...]), r.w_out_v[pl.ds(at, TILE), :], NT
        ).astype(BF)
        return 0

    lax.fori_loop(0, hidden // TILE, act_grad, 0)
    load_in.wait()
    for copy in x_copies:
        copy.wait()
    x_chain.start(0)
    g_chain.start(2) if c > 3 else None
    carried = r.grad_in.at[pl.ds(0, slots), :]
    carried[...] = jnp.zeros((slots, width), F32)

    def expert_step(t, _):
        at = pl.multiple_of(t * TILE, TILE)
        cols = pl.ds(at, TILE)
        pre = dot(flat(r.x_own[...]), r.w_in_v[cols, :], NT)
        for q in range(slots // CHUNK):
            at = slice(q * CHUNK, (q + 1) * CHUNK)
            act, slope = gelu_both(pre[at])
            r.act[at, cols] = act.astype(BF)
            r.grad_pre[at, cols] = (r.grad_pre[at, cols].astype(F32) * slope).astype(BF)
        grad_pre = r.grad_pre[:, cols]
        for s in range(width // TILE):
            part_cols = slice(s * TILE, (s + 1) * TILE)
            carried[:, part_cols] += dot(grad_pre, r.w_in_v[cols, part_cols], NN)
        return 0

    lax.fori_loop(0, hidden // TILE, expert_step, 0)
    r.g_send[...] = carried[...].astype(BF).reshape(n, cap, width)
    r_copies = [blocks_out(r.g_send, r.r_recv, (r.r_ss, r.r_rs), k) for k in order]
    for copy in r_copies:
        copy.start()
    r.r_recv[me] = r.g_send[me]

    def produce(cols):
        r.x_send[:, :, cols] = (
            dot(r.act[...], r.w_out_v[:, cols], NN).astype(BF).reshape(n, cap, TILE)
        )

    tiles(width, produce)
    p_copies = [blocks_out(r.x_send, r.p_recv, (r.p_ss, r.p_rs), k) for k in order]
    for copy in p_copies:
        copy.start()
    r.p_recv[me] = r.x_send[me]
    mine_at = pl.multiple_of(grp * part, part)

    def weight_terms(act_at, x_rows, g_rows, first):
        def one(out):
            from_act = pl.ds(pl.multiple_of(act_at + out.start, TILE), TILE)

            def two(cols):
                term_in = dot(r.grad_pre[:, from_act], x_rows(cols), TN)
                r.grad_in[out, cols] = term_in if first else r.grad_in[out, cols] + term_in
                term_out = dot(r.act[:, from_act], g_rows(cols), TN)
                r.grad_out[out, cols] = term_out if first else r.grad_out[out, cols] + term_out

            tiles(width, two)

        tiles(part, one)

    weight_terms(
        mine_at,
        lambda cols: flat(r.x_own[:, :, cols]),
        lambda cols: flat(r.g_own[:, :, cols]),
        True,
    )

    for copy in r_copies:
        copy.wait()
    for t in range(width // TILE):
        cols = slice(t * TILE, (t + 1) * TILE)
        r.grad_tokens[:, cols] = dot(r.place[...], flat(r.r_recv[:, :, cols]), TN)

    def store_hidden(at, grad_in):
        grad_hidden = r.cotangent[at, :].astype(F32) + grad_in
        r.grad_tokens[at, :] = grad_hidden
        r.block_out[at, :] = grad_hidden.astype(BF)

    sums = norm_back(r.hidden, r.grad_tokens, r.gain_ffn, store_hidden)
    r.small_own[2:3], r.small_own[3:4] = sums
    r.small_own[4:SMALL] = jnp.zeros((SMALL - 4, width), F32)
    for t in range(width // TILE):
        block = dot(r.block_out[...], r.w_o_v[t * TILE : (t + 1) * TILE, :], NT).astype(BF)
        for e in range(TILE // own):
            r.att_recv[t * (TILE // own) + e] = block[:, e * own : (e + 1) * own]
    a_copies = [blocks_out(r.att_recv, r.grad_att, (r.b_ss, r.b_rs), k) for k in order]
    for copy in a_copies:
        copy.start()
    r.grad_att[me] = r.att_recv[me]

    wo_out, wo_in = r.space.at[pl.ds(0, width), :], r.space.at[pl.ds(width, width), :]

    def wo_term(out):
        wo_out[out, :] = dot(r.attended[:, out], r.block_out[...], TN).astype(BF)

    tiles(width, wo_term)

    def to_owner(k):
        src = r.space.at[pl.ds(pl.multiple_of(partners[k] * own, own), own), :]
        dst = r.space.at[pl.ds(pl.multiple_of(width + me * own, own), own), :]
        return to_partner(src, dst, r.w_ss.at[k], r.w_rs.at[k], k)

    for k in order:
        to_owner(k).start()
    at_me = pl.ds(pl.multiple_of(me * own, own), own)
    wo_in[at_me, :] = wo_out[at_me, :]

    for copy in p_copies:
        copy.wait()
    for t in range(width // TILE):
        cols = slice(t * TILE, (t + 1) * TILE)
        r.block_out[:, cols] = (
            r.hidden[:, cols] + dot(r.place[...], flat(r.p_recv[:, :, cols]), TN)
        ).astype(BF)

    for copy in a_copies:
        copy.wait()
    for p in range(3):
        for k in order:
            to_heads(p, k).wait_send()
    for t in range(1, n):
        home(t).wait_send()
    for i in range(n):
        both = (r.grad_att[i].astype(F32) * r.att_heads[i].astype(F32)).T
        size = own // r.heads
        deltas = [
            jnp.sum(both[h * size : (h + 1) * size], axis=0, keepdims=True) for h in range(r.heads)
        ]
        r.delta[i] = jnp.concatenate(
            deltas + [jnp.zeros((SMALL - r.heads, rows), F32)], axis=0
        )
    r.grad_q_t[...] = jnp.zeros(r.grad_q_t.shape, F32)

    def back_home(p, t):
        target = lax.rem(me + t, n)
        return send(
            r.qkv_send.at[p, target],
            r.grad_tok.at[p, me],
            r.d_ss.at[p, t],
            r.d_rs.at[p, t],
            {"ep": target},
        )

    attend_back(r, me, n)
    for p in (1, 2):
        r.grad_tok[p, me] = r.qkv_send[p, me]

    def back_step(t, _):
        attend_back(r, lax.rem(me + t, n), n)
        for p in (1, 2):
            back_home(p, t).start()
        return 0

    lax.fori_loop(1, n // 2, back_step, 0)
    if c > 2:
        x_chain.start(1)
    lax.fori_loop(n // 2, n, back_step, 0)
    for i in range(n):
        r.qkv_send[0, i] = (r.grad_q_t[i].T * ((own // r.heads) ** -0.5)).astype(BF)
    for t in range(1, n):
        back_home(0, t).start()
    r.grad_tok[0, me] = r.qkv_send[0, me]
    for stage in range(3, c - 1):
        g_chain.start(stage)
    for stage in range(2, c - 1):
        x_chain.start(stage)

    piece = width // c
    for k in order:
        to_owner(k).wait()

    def o_place(e, d):
        at = pl.ds(pl.multiple_of(e * own, own), own)
        if d is None:
            return r.o_all.at[at, :]
        return r.o_all.at[at, pl.ds(pl.multiple_of(d * piece, piece), piece)]

    def q_place(e, d):
        if d is None:
            return r.q_all.at[:, e]
        return r.q_all.at[:, e, pl.ds(pl.multiple_of(d * piece, piece), piece), :]

    o_spread = Spread(r, "wo", me, grp, n, c, o_place)
    q_spread = Spread(r, "wq", me, grp, n, c, q_place)
    total = wo_in[0:own, :].astype(F32)
    for e in range(1, n):
        total = total + wo_in[e * own : (e + 1) * own, :].astype(F32)
    for d in range(c):
        r.wo_send[d] = total[:, d * piece : (d + 1) * piece].astype(BF)
    o_spread.scatter()

    for k in direct:
        pass_on(k).wait()
        gather(k).wait_send()
    gather(1).wait()
    mine.wait()
    at_once = width // rows
    turns = n // at_once

    def normed_loads(t):
        out = []
        for b in range(turns):
            spot = (t if turns <= 2 else b // 2) * TILE
            for s in range(at_once):
                out.append(
                    pltpu.make_async_copy(
                        r.normed_all.at[b * at_once + s, :, pl.ds(t * TILE, TILE)],
                        r.space.at[
                            pl.ds((b % 2) * width + s * rows, rows), pl.ds(spot, TILE)
                        ],
                        r.slab_sem.at[t % 2, b * at_once + s],
                    )
                )
        return out

    for t in range(width // TILE if turns <= 2 else 1):
        for load in normed_loads(t):
            load.start()
    for t in range(width // TILE):
        if turns > 2 and t:
            for load in normed_loads(t):
                load.start()
        for load in normed_loads(t):
            load.wait()
        total = None
        for b in range(turns):
            spot = (t if turns <= 2 else b // 2) * TILE
            grads = jnp.concatenate(
                [flat(r.qkv_send[p, b * at_once : (b + 1) * at_once]) for p in range(3)], axis=1
            )
            term = dot(
                r.space[(b % 2) * width : (b % 2 + 1) * width, spot : spot + TILE], grads, TN
            )
            total = term if b == 0 else total + term
        low = total.astype(BF)
        for s in range(TILE // piece):
            for p in range(3):
                r.wq_send[t * (TILE // piece) + s, p] = low[
                    s * piece : (s + 1) * piece, p * own : (p + 1) * own
                ]
    q_spread.scatter()
    last_loads = load_qkv(0)
    for load in last_loads:
        load.start()

    g_chain.finish()
    x_chain.finish()

    def slab_loads(q):
        at = lax.rem(grp + q, c)
        base = (q % 2) * width
        out = []
        for which, src in enumerate((r.x_all, r.g_all)):
            for s in range(n):
                out.append(
                    pltpu.make_async_copy(
                        src.at[at, s],
                        r.space.at[pl.ds(base + which * slots + s * cap, cap), :],
                        r.slab_sem.at[q % 2, which * n + s],
                    )
                )
        return out

    def slab(q):
        base = (q % 2) * width
        for load in slab_loads(q):
            load.wait()
        if q + 1 < c:
            for load in slab_loads(q + 1):
                load.start()
        x_rows, g_rows = r.space.at[pl.ds(base, slots), :], r.space.at[pl.ds(base + slots, slots), :]

        def activate(out):
            at = pl.ds(pl.multiple_of(mine_at + out.start, TILE), TILE)
            cols = pl.ds(pl.multiple_of(3 * width + out.start, TILE), TILE)
            r.grad_pre[:, cols] = dot(g_rows[...], r.w_out_v[at, :], NT).astype(BF)
            pre = dot(x_rows[...], r.w_in_v[at, :], NT)
            for q in range(slots // CHUNK):
                some = slice(q * CHUNK, (q + 1) * CHUNK)
                act, slope = gelu_both(pre[some])
                r.act[some, cols] = act.astype(BF)
                r.grad_pre[some, cols] = (r.grad_pre[some, cols].astype(F32) * slope).astype(BF)

        tiles(part, activate)
        weight_terms(
            3 * width, lambda cols: x_rows[:, cols], lambda cols: g_rows[:, cols], False
        )

    for load in slab_loads(1):
        load.start()
    o_spread.total()
    slab(1)
    q_spread.total()

    for p in (1, 2, 0):
        for t in range(1, n):
            back_home(p, t).wait_recv()
    for load in last_loads:
        load.wait()
    for p in range(3):
        for e in range(n):
            r.attended[:, e * own : (e + 1) * own] = r.grad_tok[p, e]
        cols = slice(p * width, (p + 1) * width)
        for at, weight in enumerate((r.act, r.grad_pre)):
            out = slice(at * half, (at + 1) * half)
            term = dot(r.attended[...], weight[:, cols], NT)
            r.hidden[:, out] = term if p == 0 else r.hidden[:, out] + term

    def store_tokens(at, grad_in):
        r.grad_tokens[at, :] += grad_in

    sums = norm_back(r.tokens, r.hidden, r.gain_attn, store_tokens)
    r.small_own[0:1], r.small_own[1:2] = sums

    def small_ep(k):
        return to_partner(r.small_own, r.small_ep.at[me], r.s_ss.at[0, k], r.s_rs.at[0, k], k)

    def small_dp(t):
        return send(
            r.small_sum,
            r.small_dp.at[grp],
            r.s_ss.at[1, t],
            r.s_rs.at[1, t],
            {"dp": lax.rem(grp + t, c)},
        )

    for k in order:
        small_ep(k).start()
    r.small_ep[me] = r.small_own[...]
    o_spread.over()
    for q in range(2, c):
        slab(q)
        if q == 2:
            q_spread.over()
            o_spread.share()
    if c <= 2:
        q_spread.over()
        o_spread.share()
    for k in order:
        small_ep(k).wait()
    total = r.small_ep[0]
    for e in range(1, n):
        total = total + r.small_ep[e]
    r.small_sum[...] = total
    for t in range(1, c):
        small_dp(t).start()
    r.small_dp[grp] = total
    q_spread.share()
    for t in range(1, c):
        small_dp(t).wait()
    total = r.small_dp[0]
    for d in range(1, c):
        total = total + r.small_dp[d]
    r.small[...] = total
    o_spread.finish()
    q_spread.finish()
    for p in range(3):
        for t in range(1, n):
            back_home(p, t).wait_send()


def block_call(n, c, heads, operands):
    rows, width = operands["tokens"].shape
    hidden = operands["w_in"].shape[1]
    own, cap, part, piece = width // n, 2 * rows // n, hidden // c, width // c
    slots = n * cap
    vm, hb = pl.BlockSpec(memory_space=pltpu.VMEM), pl.BlockSpec(memory_space=pl.ANY)
    sm = pl.BlockSpec(memory_space=pltpu.SMEM)
    inputs = dict(
        lengths=sm, ids=vm, tokens=vm, cotangent=vm, gain_attn=vm, shift_attn=vm, gain_ffn=vm,
        shift_ffn=vm, w_qkv=hb, w_o=hb, w_in=hb, w_out=hb,
    )
    outputs = dict(
        block_out=((rows, width), BF, vm),
        grad_tokens=((rows, width), F32, vm),
        q_all=((3, n, width, own), BF, hb),
        o_all=((width, width), BF, hb),
        small=((SMALL, width), F32, vm),
        grad_in=((part, width), F32, vm),
        grad_out=((part, width), F32, vm),
        g_all=((c, n, cap, width), BF, hb),
        x_all=((c, n, cap, width), BF, hb),
        normed_all=((n, rows, width), BF, hb),
    )

    def v(*shape):
        return pltpu.VMEM(shape, BF)

    def f(*shape):
        return pltpu.VMEM(shape, F32)

    def d(*shape):
        return pltpu.SemaphoreType.DMA(shape)

    heads_shape = (n, rows, own)
    scratch = dict(
        w_o_v=v(width, width), w_in_v=v(hidden, width), w_out_v=v(hidden, width),
        act=v(slots, hidden), grad_pre=v(slots, hidden), space=v(2 * width, width),
        normed=v(rows, width), place=v(slots, rows), hidden=f(rows, width),
        attended=v(rows, width),
        qkv_send=v(3, *heads_shape), qkv_heads=v(3, *heads_shape), grad_tok=v(3, *heads_shape),
        values_t=v(n, own, rows), att_heads=v(*heads_shape), att_recv=v(*heads_shape),
        grad_att=v(*heads_shape), grad_q_t=f(n, own, rows),
        lse=f(n, SMALL, rows), delta=f(n, SMALL, rows),
        g_send=v(n, cap, width), x_send=v(n, cap, width), g_own=v(n, cap, width),
        x_own=v(n, cap, width), r_recv=v(n, cap, width), p_recv=v(n, cap, width),
        wo_send=v(c, own, piece), wo_recv=v(c, own, piece), wo_fin=v(own, piece),
        wq_send=v(c, 3, piece, own), wq_recv=v(c, 3, piece, own),
        wq_fin=v(3, piece, own),
        small_own=f(SMALL, width), small_ep=f(n, SMALL, width), small_sum=f(SMALL, width),
        small_dp=f(c, SMALL, width),
        load_sem=d(8), slab_sem=d(2, 2 * n),
        a_ss=d(3, n), a_rs=d(3, n), g_ss=d(n), g_rs=d(n), n_ss=d(n), n_rs=d(n),
        o_ss=d(n), o_rs=d(n), x_ss=d(n), x_rs=d(n), r_ss=d(n), r_rs=d(n), p_ss=d(n), p_rs=d(n),
        b_ss=d(n), b_rs=d(n), w_ss=d(n), w_rs=d(n), d_ss=d(3, n), d_rs=d(3, n),
        gz_ss=d(2, c), gz_rs=d(2, c), xz_ss=d(2, c), xz_rs=d(2, c),
        wo_ss=d(2, c), wo_rs=d(2, c), wo_ys=d(n), wo_yr=d(n),
        wq_ss=d(2, c), wq_rs=d(2, c), wq_ys=d(n), wq_yr=d(n),
        s_ss=d(2, max(n, c)), s_rs=d(2, max(n, c)),
    )
    names = list(inputs) + list(outputs) + list(scratch)

    def kernel(*refs):
        r = types.SimpleNamespace(**dict(zip(names, refs)))
        r.heads, r.wo_slot, r.wq_slot = heads, 6, 7
        block_kernel(r, n, c)

    result = pl.pallas_call(
        kernel,
        out_shape=[jax.ShapeDtypeStruct(shape, kind) for shape, kind, _ in outputs.values()],
        in_specs=list(inputs.values()),
        out_specs=[spec for _, _, spec in outputs.values()],
        scratch_shapes=list(scratch.values()),
        compiler_params=pltpu.CompilerParams(
            collective_id=0, has_side_effects=True, vmem_limit_bytes=VMEM_LIMIT
        ),
    )(*[operands[name] for name in inputs])
    return dict(zip(outputs, result))


VMEM_LIMIT = 64 << 20


def on_device(
    tokens,
    gain_attn,
    shift_attn,
    w_qkv,
    w_o,
    gain_ffn,
    shift_ffn,
    w_in,
    w_out,
    seq_lengths,
    expert_ids,
    cotangent,
):
    rows, width = tokens.shape
    n, c = lax.axis_size("ep"), lax.axis_size("dp")
    operands = dict(
        lengths=seq_lengths,
        ids=expert_ids.reshape(1, rows),
        tokens=tokens,
        cotangent=cotangent,
        gain_attn=gain_attn[None],
        shift_attn=shift_attn[None],
        gain_ffn=gain_ffn[None],
        shift_ffn=shift_ffn[None],
        w_qkv=w_qkv,
        w_o=w_o,
        w_in=w_in,
        w_out=w_out,
    )
    out = block_call(n, c, HEADS // n, operands)
    grad_w_qkv = out["q_all"].transpose(2, 0, 1, 3).reshape(width, 3 * width).astype(F32)
    grad_w_o = out["o_all"].astype(F32)
    small = out["small"]
    return (
        out["block_out"],
        out["grad_tokens"],
        grad_w_qkv,
        grad_w_o,
        small[0],
        small[1],
        small[2],
        small[3],
        out["grad_in"][None],
        out["grad_out"][None],
    )


def solution(mesh):
    return jax.shard_map(
        on_device,
        mesh=mesh,
        in_specs=(
            P(("dp", "ep"), None),
            P(),
            P(),
            P(),
            P(),
            P(),
            P(),
            P("ep", None, None),
            P("ep", None, None),
            P("dp", None),
            P(("dp", "ep"), None),
            P(("dp", "ep"), None),
        ),
        out_specs=(
            P(("dp", "ep"), None),
            P(("dp", "ep"), None),
            P(),
            P(),
            P(),
            P(),
            P(),
            P(),
            P("ep", "dp", None),
            P("ep", "dp", None),
        ),
        check_vma=False,
    )
```

time: 618 us -> 335 us (0.54)
  Pallas kernels: 51.9 us -> 284 us
  waiting for transfers between devices: 219 us -> 0 us
  matrix products: 118 us -> 0 us
  blocking collectives: 72.5 us -> 0 us
  local copies, waits for them, and re-layouts: 86.3 us -> 34.3 us
  starting transfers between devices: 26.4 us -> 0 us
  between operations: 14.9 us -> 0.68 us
  other arithmetic: 21.6 us -> 11.6 us
    pallas_call x2 -> x1, Pallas kernels: 51.9 us -> 284 us  [block_call(): pl.pallas_call(kernel, out_shape=[jax.ShapeDtypeStruct(shape, kind) for s...]
    dot_general x16 -> x0, matrix products: 118 us -> none  [the longest x6 44 us: contract_rows(): lax.dot_general(left, right, (((0,), (0,)), ((), ())), preferred_element_...]
    all_gather x5 -> x0, waiting for transfers between devices: 106 us -> none  [the longest x1 58.4 us: on_device(): both = lax.all_gather(both, ('dp', 'ep'), axis=0, tiled=True)]
    all_to_all x6 -> x0, waiting for transfers between devices: 83.5 us -> none  [exchange(): return lax.all_to_all(blocks, 'ep', split_axis=0, concat_axis=0, tiled=True)]
    psum x1 -> x0, blocking collectives: 38.5 us -> none  [on_device(): lax.psum((grad_gain_attn, grad_shift_attn, grad_gain_ffn, grad_shift_ffn)...]
    all_to_all x2 -> x0, blocking collectives: 34 us -> none  [exchange(): return lax.all_to_all(blocks, 'ep', split_axis=0, concat_axis=0, tiled=True)]
    transpose x5 -> x0, local copies, waits for them, and re-layouts: 32.3 us -> none  [the longest x2 24.7 us: on_device(): both[:, :, :, :3].transpose(0, 2, 3, 1, 4).reshape(width, 3 * width)]
    reduce_scatter x1 -> x0, waiting for transfers between devices: 27.4 us -> none  [on_device(): both = lax.psum_scatter(both, 'dp', scatter_dimension=0, tiled=True)]
  transfers between devices with their start and end apart: 12 -> 0, of which waited for: 9 -> 0; matrix products, arithmetic and copies ran while one was open for 21% -> 0% of each run, Pallas kernels for 9% -> 0%
where the time goes in v2:
time: 335 us; the launch traced here: 331 us
  Pallas kernels  284 us (85%)
  local copies, waits for them, and re-layouts  34.3 us (10%)
  other arithmetic  11.6 us (3%)
    pallas_call x1, Pallas kernels, block_call(): pl.pallas_call(kernel, out_shape=[jax.ShapeDtypeStruct(shape, kind) for s...  284 us
    unnamed x15, local copies, waits for them, and re-layouts  20.2 us
    convert_element_type x1, local copies, waits for them, and re-layouts, on_device(): out['q_all'].transpose(2, 0, 1, 3).reshape(width, 3 * width).astype(F32)  12.5 us
    convert_element_type x1, other arithmetic, on_device(): out['q_all'].transpose(2, 0, 1, 3).reshape(width, 3 * width).astype(F32)  9 us

profile of v2, /device:TPU:0, one launch (start us, length us, event | category | flops | bytes accessed | tf_op | source)
XLA Modules:
  0.0 330.7 jit_solution(4201651762473188887)
XLA Ops:
  0.6 284.1 %shard_map.195 = (bf16[256,1024]{1,0:T(8,128)(2,1)}, f32[256,1024]{1,0:T(8,128)}, bf16[3,8,1024,128]{3,2,1,0:T(8,128)(2,1)}, bf16[1024,1024]{1,0:T(8,128)(2,1)},...) custom-call(s32[1,4]{1,0:T(1,128)} %refs_0_.1, ...), custom_call_target="tpu_custom_call" | custom-call | tf_op jit(solution)/shard_map/pallas_call | solution.py:953
  284.8 1.6 fusion
  286.3 9.0 %convert_bitcast_fusion = f32[1024,3,8,128]{3,0,2,1:T(8,128)} fusion(bf16[3,8,1024,128]{3,2,1,0:T(8,128)(2,1)} %get-tuple-element.19), kind=kLoop, calls=%fused_computation | loop fusion | flops 3145728 | bytes 18874368 | tf_op jit(solution)/shard_map/convert_element_type | solution.py:1000
  295.3 12.5 %copy.22 = f32[1024,3,8,128]{0,3,2,1:T(8,128)} copy(f32[1024,3,8,128]{3,0,2,1:T(8,128)} %convert_bitcast_fusion) | data formatting | bytes 25165824 | tf_op jit(solution)/shard_map/convert_element_type | solution.py:1000
  307.9 0.0 copy-start.2
  307.9 12.8 %copy.23 = f32[1024,3072]{1,0:T(8,128)} copy(f32[1024,3072]{0,1:T(8,128)} %bitcast.14) | data formatting | bytes 25165824
  320.6 0.0 copy-start.4
  320.6 0.0 copy-start.3
  320.6 0.0 copy-done.2
  320.6 0.0 copy-start.1
  320.6 2.6 convert_element_type.15
  323.2 0.0 copy-done.4
  323.2 0.8 copy.28
  324.0 0.0 copy-done.3
  324.0 1.0 copy.29
  325.0 0.0 copy-done.1
  325.0 0.0 copy-start
  325.0 2.1 copy.30
  327.1 1.6 copy-done
  328.7 2.0 copy.31
Async XLA Ops:
  307.9 12.8 %copy-start.2 = (bf16[1024,1024]{1,0:T(8,128)(2,1)S(1)}, bf16[1024,1024]{1,0:T(8,128)(2,1)}, u32[]{:S(2)}) copy-start(bf16[1024,1024]{1,0:T(8,128)(2,1)} %get-tuple-element.20) | copy-start | bytes 6291460
  320.6 2.6 copy-start.4
  320.6 3.4 %copy-start.3 = (f32[256,1024]{1,0:T(8,128)S(1)}, f32[256,1024]{1,0:T(8,128)}, u32[]{:S(2)}) copy-start(f32[256,1024]{1,0:T(8,128)} %get-tuple-element.49) | copy-start | bytes 3145732
  320.6 4.4 %copy-start.1 = (f32[1024,1024]{1,0:T(8,128)S(1)}, f32[1024,1024]{1,0:T(8,128)}, u32[]{:S(2)}) copy-start(f32[1024,1024]{1,0:T(8,128)} %get-tuple-element.22) | copy-start | bytes 12582916
  325.0 3.7 %copy-start = (f32[1024,1024]{1,0:T(8,128)S(1)}, f32[1024,1024]{1,0:T(8,128)}, u32[]{:S(2)}) copy-start(f32[1024,1024]{1,0:T(8,128)} %get-tuple-element.23) | copy-start | bytes 12582916

commit v3 on v2

--- a/solution.py
+++ b/solution.py
@@ -13,6 +13,8 @@
 MASKED = -1e30
 TILE = 512
 SMALL = 8
+UNROLLED = 8
+AT_ONCE = 4
 MESH = pl.DeviceIdType.MESH
 F32 = jnp.float32
 BF = jnp.bfloat16
@@ -151,6 +153,91 @@
 
 
 def attend_block(r, i):
+    rows, own = r.qkv_heads.shape[2:]
+    heads = r.heads
+    size = own // heads
+    queries = split_heads(r.qkv_heads[0, i] * BF(size**-0.5), heads)
+    pos, start = start_row(r.lengths, i * rows, rows)
+    outs, sums = [], []
+    for h in range(heads):
+        top = jnp.full((1, rows), MASKED, F32)
+        total = jnp.zeros((1, rows), F32)
+        accum = jnp.zeros((size, rows), F32)
+        for last in range(i, -1, -AT_ONCE):
+            scores = []
+            blocks = range(last, max(last - AT_ONCE, -1), -1)
+            for j in blocks:
+                key = j * rows + lax.broadcasted_iota(jnp.int32, (rows, rows), 0)
+                allowed = key >= start
+                if j == i:
+                    allowed = allowed & (key <= pos)
+                scores.append(
+                    jnp.where(allowed, dot(r.qkv_heads[1, j], queries[h], NT), MASKED)
+                )
+            peak = functools.reduce(
+                jnp.maximum, [jnp.max(s.reshape(rows // 8, 8, rows), axis=0) for s in scores]
+            )
+            new_top = jnp.maximum(top, jnp.max(peak, axis=0, keepdims=True))
+            decay = jnp.exp(top - new_top)
+            accum = accum * decay
+            part = jnp.zeros((8, rows), F32)
+            for j, s in zip(blocks, scores):
+                weights = jnp.exp(s - new_top)
+                part = part + jnp.sum(weights.reshape(rows // 8, 8, rows), axis=0)
+                values = r.values_t[j, h * size : (h + 1) * size, :]
+                accum = accum + dot(values, weights.astype(BF), NN)
+            total = total * decay + jnp.sum(part, axis=0, keepdims=True)
+            top = new_top
+        outs.append(accum / total)
+        sums.append(top + jnp.log(total))
+    r.att_heads[i] = jnp.concatenate(outs, axis=0).T.astype(BF)
+    r.lse[i] = jnp.concatenate(sums + [jnp.zeros((SMALL - heads, rows), F32)], axis=0)
+
+
+def attend_back(r, j, n):
+    rows, own = r.qkv_heads.shape[2:]
+    heads = r.heads
+    size = own // heads
+    keys, values = r.qkv_heads[1, j], r.qkv_heads[2, j]
+    keys_t = keys.astype(F32).T.astype(BF)
+
+    def fold(at, carry, diagonal):
+        grad_k, grad_v = carry
+        for i in at:
+            queries = split_heads(r.qkv_heads[0, i] * BF(size**-0.5), heads)
+            grads = split_heads(r.grad_att[i], heads)
+            pos, start = start_row(r.lengths, i * rows, rows)
+            key = j * rows + lax.broadcasted_iota(jnp.int32, (rows, rows), 0)
+            allowed = key >= start
+            if diagonal:
+                allowed = allowed & (key <= pos)
+            for h in range(heads):
+                scores = dot(keys, queries[h], NT)
+                probs = jnp.where(allowed, jnp.exp(scores - r.lse[i, h : h + 1, :]), 0.0)
+                grad_probs = dot(values, grads[h], NT)
+                grad_scores = (probs * (grad_probs - r.delta[i, h : h + 1, :])).astype(BF)
+                grad_v = grad_v + dot(probs.astype(BF), grads[h], NN)
+                grad_k = grad_k + dot(grad_scores, queries[h], NN)
+                part = slice(h * size, (h + 1) * size)
+                r.grad_q_t[i, part, :] += dot(keys_t[part, :], grad_scores, NN)
+        return grad_k, grad_v
+
+    zero = jnp.zeros((rows, own), F32)
+    carry = fold([j], (zero, zero), True)
+    left = n - 1 - j
+    odd = lax.rem(left, 2)
+    carry = lax.fori_loop(j + 1, j + 1 + odd, lambda i, carry: fold([i], carry, False), carry)
+
+    def pair(t, carry):
+        i = j + 1 + odd + 2 * t
+        return fold([i, i + 1], carry, False)
+
+    grad_k, grad_v = lax.fori_loop(0, lax.div(left, 2), pair, carry)
+    r.qkv_send[1, j] = grad_k.astype(BF)
+    r.qkv_send[2, j] = grad_v.astype(BF)
+
+
+def attend_block_loop(r, i):
     rows, own = r.qkv_heads.shape[2:]
     heads = r.heads
     size = own // heads
@@ -194,103 +281,133 @@
     r.lse[i] = jnp.concatenate(sums + [jnp.zeros((SMALL - heads, rows), F32)], axis=0)
 
 
-def attend_back(r, j, n):
-    rows, own = r.qkv_heads.shape[2:]
-    heads = r.heads
-    size = own // heads
-    keys, values = r.qkv_heads[1, j], r.qkv_heads[2, j]
-    keys_t = keys.astype(F32).T.astype(BF)
-
-    def fold(i, carry, diagonal):
-        grad_k, grad_v = carry
-        queries = split_heads(r.qkv_heads[0, i] * BF(size**-0.5), heads)
-        grads = split_heads(r.grad_att[i], heads)
-        pos, start = start_row(r.lengths, i * rows, rows)
-        key = j * rows + lax.broadcasted_iota(jnp.int32, (rows, rows), 0)
-        allowed = key >= start
-        if diagonal:
-            allowed = allowed & (key <= pos)
-        for h in range(heads):
-            scores = dot(keys, queries[h], NT)
-            probs = jnp.where(allowed, jnp.exp(scores - r.lse[i, h : h + 1, :]), 0.0)
-            grad_probs = dot(values, grads[h], NT)
-            grad_scores = (probs * (grad_probs - r.delta[i, h : h + 1, :])).astype(BF)
-            grad_v = grad_v + dot(probs.astype(BF), grads[h], NN)
-            grad_k = grad_k + dot(grad_scores, queries[h], NN)
-            part = slice(h * size, (h + 1) * size)
-            r.grad_q_t[i, part, :] += dot(keys_t[part, :], grad_scores, NN)
-        return grad_k, grad_v
-
-    zero = jnp.zeros((rows, own), F32)
-    carry = fold(j, (zero, zero), True)
-    grad_k, grad_v = lax.fori_loop(
-        j + 1, n, lambda i, carry: fold(i, carry, False), carry
-    )
-    r.qkv_send[1, j] = grad_k.astype(BF)
-    r.qkv_send[2, j] = grad_v.astype(BF)
-
-
-class Chain:
+class Line:
     def __init__(self, block, whole, send_sem, recv_sem, at, c):
         self.block, self.whole, self.at, self.c = block, whole, at, c
         self.send_sem, self.recv_sem = send_sem, recv_sem
 
-    def copy(self, way, stage):
-        held = self.at - stage if way == 0 else self.at + stage
-        target = self.at + 1 if way == 0 else self.at - 1
-        src = self.block if stage == 0 else self.whole.at[held]
+    def direct(self, way, hops):
+        target = self.at + way * hops
+        return self.can(target), send(
+            self.block,
+            self.whole.at[self.at],
+            self.send_sem.at[(way + 1) // 2, hops - 1],
+            self.recv_sem.at[self.at],
+            {"dp": target},
+        )
+
+    def can(self, index):
+        return (index >= 0) & (index < self.c)
+
+    def onward(self, way, stage):
+        held = self.at - way * (2 + stage)
+        target = self.at + way
+        src = self.whole.at[held]
+        return self.can(held) & self.can(target), send(
+            src,
+            src,
+            self.send_sem.at[(way + 1) // 2, 2 + stage],
+            self.recv_sem.at[held],
+            {"dp": target},
+        )
+
+    def start(self):
+        for hops in range(1, min(3, self.c)):
+            for way in (-1, 1):
+                allowed, copy = self.direct(way, hops)
+                pl.when(allowed)(copy.start)
+
+    def hand_on(self):
+        for stage in range(self.c - 3):
+            for way in (-1, 1):
+                allowed, copy = self.onward(way, stage)
+
+                @pl.when(allowed)
+                def _():
+                    copy.wait_recv()
+                    copy.start()
+
+    def wait(self, block):
+        away = block - self.at
+        below, above = away < -1, away > 1
+        done = (below & self.can(self.at + 1)) | (above & self.can(self.at - 1))
+
+        @pl.when(jnp.logical_not(done))
+        def _():
+            src = self.whole.at[block]
+            send(src, src, self.send_sem.at[0, 0], self.recv_sem.at[block], {"dp": block}).wait_recv()
+
+    def finish(self):
+        for way in (-1, 1):
+            for hops in range(1, min(3, self.c)):
+                allowed, copy = self.direct(way, hops)
+                pl.when(allowed)(copy.wait_send)
+            for stage in range(self.c - 3):
+                allowed, copy = self.onward(way, stage)
+                pl.when(allowed)(copy.wait_send)
+
+
+class Gather:
+    def __init__(self, own, place, halves, send_sem, recv_sem, me, n):
+        self.own, self.place, self.halves = own, place, halves
+        self.send_sem, self.recv_sem, self.me, self.n = send_sem, recv_sem, me, n
+        self.direct = [k for k in order_of(n) if k % 2 == 0]
+        self.relayed = n == 8
+        self.near = [2, 4] if self.relayed else self.direct
+
+    def to(self, src, dst, at, k):
         return send(
-            src,
-            self.whole.at[held],
-            self.send_sem.at[way, stage],
-            self.recv_sem.at[way, stage],
-            {"dp": target},
-        )
-
-    def sends(self, way, stage):
-        if way == 0:
-            return (self.at >= stage) & (self.at + 1 < self.c)
-        return (self.at + stage < self.c) & (self.at >= 1)
-
-    def gets(self, way, stage):
-        return self.at >= stage + 1 if way == 0 else self.at + stage + 1 < self.c
-
-    def start(self, stage):
-        for way in range(2):
-            if stage:
-
-                @pl.when(self.gets(way, stage - 1))
-                def _():
-                    self.copy(way, stage - 1).wait_recv()
-
-            @pl.when(self.sends(way, stage))
-            def _():
-                self.copy(way, stage).start()
+            src, dst, self.send_sem.at[at], self.recv_sem.at[at], {"ep": partner(self.me, k, self.n)}
+        )
+
+    def across(self, k):
+        return self.to(self.own, self.place(self.me), k, k)
+
+    def relay(self, k):
+        half = self.halves(partner(self.me, k, self.n))[k // 4]
+        return self.to(half, half, self.n + k // 4, 6 - k)
+
+    def pass_on(self, k):
+        block = self.place(partner(self.me, k, self.n))
+        return self.to(block, block, k + 1, 1)
+
+    def start(self):
+        for k in self.near + [1]:
+            self.across(k).start()
+
+    def middle(self):
+        for k in self.near:
+            self.across(k).wait_recv()
+            if self.relayed:
+                self.relay(k).start()
+            self.pass_on(k).start()
+
+    def last(self):
+        if self.relayed:
+            for k in (2, 4):
+                self.relay(k).wait_recv()
+            self.pass_on(6).start()
 
     def finish(self):
-        for way in range(2):
-
-            @pl.when(self.gets(way, self.c - 2))
-            def _():
-                self.copy(way, self.c - 2).wait_recv()
-
-            for stage in range(self.c - 1):
-
-                @pl.when(self.sends(way, stage))
-                def _():
-                    self.copy(way, stage).wait_send()
+        self.across(1).wait()
+        for k in self.near:
+            self.across(k).wait_send()
+            if self.relayed:
+                self.relay(k).wait_send()
+        for k in self.direct:
+            self.pass_on(k).wait()
 
 
 class Spread:
-    def __init__(self, r, name, me, grp, n, c, place):
-        self.send_buf, self.recv_buf, self.final = (
-            getattr(r, name + part) for part in ("_send", "_recv", "_fin")
-        )
-        self.ss, self.rs = getattr(r, name + "_ss"), getattr(r, name + "_rs")
-        self.ys, self.yr = getattr(r, name + "_ys"), getattr(r, name + "_yr")
-        self.me, self.grp, self.n, self.c, self.place = me, grp, n, c, place
-        self.local = r.load_sem.at[getattr(r, name + "_slot")]
-        self.direct = [k for k in order_of(n) if k % 2 == 0]
+    def __init__(self, r, name, me, grp, n, c, place, halves):
+        self.send_buf, self.recv_buf, self.final, self.ss, self.rs, ys, yr, self.local = (
+            getattr(r, name + part)
+            for part in ("_send", "_recv", "_fin", "_ss", "_rs", "_ys", "_yr", "_ls")
+        )
+        self.me, self.grp, self.c, self.place = me, grp, c, place
+        self.gather = Gather(
+            place(me, None), lambda e: place(e, None), halves, ys, yr, me, n
+        )
 
     def to_piece(self, t):
         target = lax.rem(self.grp + t, self.c)
@@ -311,20 +428,9 @@
             {"dp": lax.rem(self.grp + t, self.c)},
         )
 
-    def across(self, k):
-        block = self.place(self.me, None)
-        return send(
-            block, block, self.ys.at[k], self.yr.at[k], {"ep": partner(self.me, k, self.n)}
-        )
-
-    def pass_on(self, k):
-        block = self.place(partner(self.me, k, self.n), None)
-        return send(
-            block,
-            block,
-            self.ys.at[k + 1],
-            self.yr.at[k + 1],
-            {"ep": partner(self.me, 1, self.n)},
+    def mine(self):
+        return pltpu.make_async_copy(
+            self.final, self.place(self.me, self.grp), self.local.at[0]
         )
 
     def scatter(self):
@@ -341,28 +447,16 @@
         self.final[...] = total.astype(BF)
         for t in range(1, self.c):
             self.to_copies(t).start()
-        self.mine = pltpu.make_async_copy(
-            self.final, self.place(self.me, self.grp), self.local
-        )
-        self.mine.start()
+        self.mine().start()
 
     def over(self):
         for t in range(1, self.c):
             self.to_copies(t).wait_recv()
-        self.mine.wait()
-        for k in self.direct + [1]:
-            self.across(k).start()
-
-    def share(self):
-        for k in self.direct:
-            self.across(k).wait_recv()
-            self.pass_on(k).start()
+        self.mine().wait()
+        self.gather.start()
 
     def finish(self):
-        self.across(1).wait()
-        for k in self.direct:
-            self.across(k).wait_send()
-            self.pass_on(k).wait()
+        self.gather.finish()
         for t in range(1, self.c):
             self.to_piece(t).wait_send()
             self.to_copies(t).wait_send()
@@ -412,8 +506,19 @@
     for load in first_loads + [load_o, load_out, load_in]:
         load.start()
 
+    r.place[...] = place_matrix(r.ids[...], n, cap)
+    for t in range(width // TILE):
+        cols = slice(t * TILE, (t + 1) * TILE)
+        r.g_send[:, :, cols] = (
+            dot(r.place[...], r.cotangent[:, cols], NN).astype(BF).reshape(n, cap, TILE)
+        )
+    pl.semaphore_wait(barrier, n - 1 + c - 1)
+    g_copies = [blocks_out(r.g_send, r.g_own, (r.g_ss, r.g_rs), k) for k in order]
+    for copy in g_copies:
+        copy.start()
+    r.g_own[me] = r.g_send[me]
+
     norm_apply(r.tokens, r.gain_attn, r.shift_attn, r.normed)
-    pl.semaphore_wait(barrier, n - 1 + c - 1)
 
     def to_heads(p, k):
         return to_partner(
@@ -437,29 +542,27 @@
             to_heads(p, k).start()
         r.qkv_heads[p, me] = r.qkv_send[p, me]
 
-    r.place[...] = place_matrix(r.ids[...], n, cap)
-    for t in range(width // TILE):
-        cols = slice(t * TILE, (t + 1) * TILE)
-        r.g_send[:, :, cols] = (
-            dot(r.place[...], r.cotangent[:, cols], NN).astype(BF).reshape(n, cap, TILE)
-        )
+    g_line = Line(r.g_own, r.g_all, r.gz_ss, r.gz_rs, grp, c)
+    x_line = Line(r.x_own, r.x_all, r.xz_ss, r.xz_rs, grp, c)
+    for copy in g_copies:
+        copy.wait()
+    g_line.start()
+
+    load_out.wait()
+
     for p in range(3):
         for k in order:
             to_heads(p, k).wait_recv()
-    g_copies = [blocks_out(r.g_send, r.g_own, (r.g_ss, r.g_rs), k) for k in order]
-    for copy in g_copies:
-        copy.start()
-    r.g_own[me] = r.g_send[me]
-
-    def gather(k):
-        return to_partner(r.normed, r.normed_all.at[me], r.n_ss.at[k], r.n_rs.at[k], k)
-
-    def pass_on(k):
-        src = r.normed_all.at[partners[k]]
-        return to_partner(src, src, r.n_ss.at[k + 1], r.n_rs.at[k + 1], 1)
-
-    for k in direct + [1]:
-        gather(k).start()
+
+    def normed_halves(e):
+        return [
+            r.normed_all.at[e, pl.ds(0, rows // 2), :],
+            r.normed_all.at[e, pl.ds(rows // 2, rows // 2), :],
+        ]
+
+    normed_gather = Gather(
+        r.normed, lambda e: r.normed_all.at[e], normed_halves, r.n_ss, r.n_rs, me, n
+    )
     mine = pltpu.make_async_copy(r.normed, r.normed_all.at[me], r.load_sem.at[5])
     mine.start()
 
@@ -476,24 +579,22 @@
             {"ep": target},
         )
 
-    attend_block(r, me)
+    def block_step(t, _):
+        at = lax.rem(me + t, n)
+        if n > UNROLLED:
+            attend_block_loop(r, at)
+        else:
+            lax.switch(at, [functools.partial(attend_block, r, i) for i in range(n)])
+
+        @pl.when(t > 0)
+        def _():
+            home(t).start()
+
+        return 0
+
+    lax.fori_loop(0, n, block_step, 0)
     r.att_recv[me] = r.att_heads[me]
 
-    def block_step(t, _):
-        attend_block(r, lax.rem(me + t, n))
-        home(t).start()
-        return 0
-
-    lax.fori_loop(1, n // 2, block_step, 0)
-    for copy in g_copies:
-        copy.wait()
-    g_chain = Chain(r.g_own, r.g_all, r.gz_ss, r.gz_rs, grp, c)
-    x_chain = Chain(r.x_own, r.x_all, r.xz_ss, r.xz_rs, grp, c)
-    g_chain.start(0)
-    lax.fori_loop(n // 2, n, block_step, 0)
-    for k in direct:
-        gather(k).wait_recv()
-        pass_on(k).start()
     for t in range(1, n):
         home(t).wait_recv()
     for e in range(n):
@@ -515,43 +616,35 @@
     for copy in x_copies:
         copy.start()
     r.x_own[me] = r.x_send[me]
-    g_chain.start(1)
-
-    load_out.wait()
-
-    def act_grad(t, _):
-        at = pl.multiple_of(t * TILE, TILE)
-        r.grad_pre[:, pl.ds(at, TILE)] = dot(
-            flat(r.g_own[...]), r.w_out_v[pl.ds(at, TILE), :], NT
-        ).astype(BF)
-        return 0
-
-    lax.fori_loop(0, hidden // TILE, act_grad, 0)
+
+    def act_grad(cols):
+        r.grad_pre[:, cols] = dot(flat(r.g_own[...]), r.w_out_v[cols, :], NT).astype(BF)
+
+    tiles(hidden, act_grad)
+    g_line.hand_on()
     load_in.wait()
+
     for copy in x_copies:
         copy.wait()
-    x_chain.start(0)
-    g_chain.start(2) if c > 3 else None
-    carried = r.grad_in.at[pl.ds(0, slots), :]
-    carried[...] = jnp.zeros((slots, width), F32)
-
-    def expert_step(t, _):
-        at = pl.multiple_of(t * TILE, TILE)
-        cols = pl.ds(at, TILE)
+    x_line.start()
+    normed_gather.start()
+
+    def expert_step(cols):
         pre = dot(flat(r.x_own[...]), r.w_in_v[cols, :], NT)
         for q in range(slots // CHUNK):
             at = slice(q * CHUNK, (q + 1) * CHUNK)
             act, slope = gelu_both(pre[at])
             r.act[at, cols] = act.astype(BF)
             r.grad_pre[at, cols] = (r.grad_pre[at, cols].astype(F32) * slope).astype(BF)
-        grad_pre = r.grad_pre[:, cols]
-        for s in range(width // TILE):
-            part_cols = slice(s * TILE, (s + 1) * TILE)
-            carried[:, part_cols] += dot(grad_pre, r.w_in_v[cols, part_cols], NN)
-        return 0
-
-    lax.fori_loop(0, hidden // TILE, expert_step, 0)
-    r.g_send[...] = carried[...].astype(BF).reshape(n, cap, width)
+
+    tiles(hidden, expert_step)
+
+    def routed_grad(cols):
+        r.g_send[:, :, cols] = (
+            dot(r.grad_pre[...], r.w_in_v[:, cols], NN).astype(BF).reshape(n, cap, TILE)
+        )
+
+    tiles(width, routed_grad)
     r_copies = [blocks_out(r.g_send, r.r_recv, (r.r_ss, r.r_rs), k) for k in order]
     for copy in r_copies:
         copy.start()
@@ -563,9 +656,6 @@
         )
 
     tiles(width, produce)
-    p_copies = [blocks_out(r.x_send, r.p_recv, (r.p_ss, r.p_rs), k) for k in order]
-    for copy in p_copies:
-        copy.start()
     r.p_recv[me] = r.x_send[me]
     mine_at = pl.multiple_of(grp * part, part)
 
@@ -575,9 +665,9 @@
 
             def two(cols):
                 term_in = dot(r.grad_pre[:, from_act], x_rows(cols), TN)
-                r.grad_in[out, cols] = term_in if first else r.grad_in[out, cols] + term_in
+                r.sum_in[out, cols] = term_in if first else r.sum_in[out, cols] + term_in
                 term_out = dot(r.act[:, from_act], g_rows(cols), TN)
-                r.grad_out[out, cols] = term_out if first else r.grad_out[out, cols] + term_out
+                r.sum_out[out, cols] = term_out if first else r.sum_out[out, cols] + term_out
 
             tiles(width, two)
 
@@ -592,6 +682,9 @@
 
     for copy in r_copies:
         copy.wait()
+
+    normed_gather.middle()
+
     for t in range(width // TILE):
         cols = slice(t * TILE, (t + 1) * TILE)
         r.grad_tokens[:, cols] = dot(r.place[...], flat(r.r_recv[:, :, cols]), TN)
@@ -613,33 +706,33 @@
         copy.start()
     r.grad_att[me] = r.att_recv[me]
 
-    wo_out, wo_in = r.space.at[pl.ds(0, width), :], r.space.at[pl.ds(width, width), :]
-
-    def wo_term(out):
-        wo_out[out, :] = dot(r.attended[:, out], r.block_out[...], TN).astype(BF)
-
-    tiles(width, wo_term)
+    def wo_rows(buf, e):
+        at = e * own
+        return buf.at[
+            pl.ds(pl.multiple_of(lax.rem(at, slots), own), own),
+            pl.ds(pl.multiple_of(lax.div(at, slots) * width, width), width),
+        ]
+
+    for t in range(width // slots):
+        out = slice(t * slots, (t + 1) * slots)
+        r.act[:, t * width : (t + 1) * width] = dot(
+            r.attended[:, out], r.block_out[...], TN
+        ).astype(BF)
 
     def to_owner(k):
-        src = r.space.at[pl.ds(pl.multiple_of(partners[k] * own, own), own), :]
-        dst = r.space.at[pl.ds(pl.multiple_of(width + me * own, own), own), :]
-        return to_partner(src, dst, r.w_ss.at[k], r.w_rs.at[k], k)
-
+        return to_partner(
+            wo_rows(r.act, partners[k]), wo_rows(r.grad_pre, me), r.w_ss.at[k], r.w_rs.at[k], k
+        )
+
+    for copy in a_copies:
+        copy.wait()
+    p_copies = [blocks_out(r.x_send, r.p_recv, (r.p_ss, r.p_rs), k) for k in order]
+    for copy in p_copies:
+        copy.start()
     for k in order:
         to_owner(k).start()
-    at_me = pl.ds(pl.multiple_of(me * own, own), own)
-    wo_in[at_me, :] = wo_out[at_me, :]
-
-    for copy in p_copies:
-        copy.wait()
-    for t in range(width // TILE):
-        cols = slice(t * TILE, (t + 1) * TILE)
-        r.block_out[:, cols] = (
-            r.hidden[:, cols] + dot(r.place[...], flat(r.p_recv[:, :, cols]), TN)
-        ).astype(BF)
-
-    for copy in a_copies:
-        copy.wait()
+    wo_rows(r.grad_pre, me)[...] = wo_rows(r.act, me)[...]
+
     for p in range(3):
         for k in order:
             to_heads(p, k).wait_send()
@@ -666,58 +759,64 @@
             {"ep": target},
         )
 
-    attend_back(r, me, n)
-    for p in (1, 2):
-        r.grad_tok[p, me] = r.qkv_send[p, me]
-
     def back_step(t, _):
         attend_back(r, lax.rem(me + t, n), n)
-        for p in (1, 2):
-            back_home(p, t).start()
+
+        @pl.when(t > 0)
+        def _():
+            for p in (1, 2):
+                back_home(p, t).start()
+
         return 0
 
-    lax.fori_loop(1, n // 2, back_step, 0)
-    if c > 2:
-        x_chain.start(1)
-    lax.fori_loop(n // 2, n, back_step, 0)
+    lax.fori_loop(0, n, back_step, 0)
     for i in range(n):
         r.qkv_send[0, i] = (r.grad_q_t[i].T * ((own // r.heads) ** -0.5)).astype(BF)
     for t in range(1, n):
         back_home(0, t).start()
-    r.grad_tok[0, me] = r.qkv_send[0, me]
-    for stage in range(3, c - 1):
-        g_chain.start(stage)
-    for stage in range(2, c - 1):
-        x_chain.start(stage)
-
-    piece = width // c
-    for k in order:
-        to_owner(k).wait()
+    for p in range(3):
+        r.grad_tok[p, me] = r.qkv_send[p, me]
+    normed_gather.last()
 
     def o_place(e, d):
         at = pl.ds(pl.multiple_of(e * own, own), own)
+        piece = width // c
         if d is None:
             return r.o_all.at[at, :]
         return r.o_all.at[at, pl.ds(pl.multiple_of(d * piece, piece), piece)]
 
-    def q_place(e, d):
+    def o_halves(e):
+        at = pl.ds(pl.multiple_of(e * own, own), own)
+        return [r.o_all.at[at, pl.ds(0, half)], r.o_all.at[at, pl.ds(half, half)]]
+
+    def q_place(first, e, d):
+        piece = TILE // c
         if d is None:
-            return r.q_all.at[:, e]
-        return r.q_all.at[:, e, pl.ds(pl.multiple_of(d * piece, piece), piece), :]
-
-    o_spread = Spread(r, "wo", me, grp, n, c, o_place)
-    q_spread = Spread(r, "wq", me, grp, n, c, q_place)
-    total = wo_in[0:own, :].astype(F32)
-    for e in range(1, n):
-        total = total + wo_in[e * own : (e + 1) * own, :].astype(F32)
-    for d in range(c):
-        r.wo_send[d] = total[:, d * piece : (d + 1) * piece].astype(BF)
-    o_spread.scatter()
-
-    for k in direct:
-        pass_on(k).wait()
-        gather(k).wait_send()
-    gather(1).wait()
+            return r.q_all.at[:, e, pl.ds(first, TILE), :]
+        return r.q_all.at[:, e, pl.ds(pl.multiple_of(first + d * piece, piece), piece), :]
+
+    def q_halves(first, e):
+        return [
+            r.q_all.at[:, e, pl.ds(first, TILE // 2), :],
+            r.q_all.at[:, e, pl.ds(first + TILE // 2, TILE // 2), :],
+        ]
+
+    o_spread = Spread(r, "wo", me, grp, n, c, o_place, o_halves)
+    q_spreads = [
+        Spread(
+            r,
+            "wq" + str(t),
+            me,
+            grp,
+            n,
+            c,
+            functools.partial(q_place, t * TILE),
+            functools.partial(q_halves, t * TILE),
+        )
+        for t in range(width // TILE)
+    ]
+
+    normed_gather.finish()
     mine.wait()
     at_once = width // rows
     turns = n // at_once
@@ -741,7 +840,7 @@
     for t in range(width // TILE if turns <= 2 else 1):
         for load in normed_loads(t):
             load.start()
-    for t in range(width // TILE):
+    for t, spread in enumerate(q_spreads):
         if turns > 2 and t:
             for load in normed_loads(t):
                 load.start()
@@ -758,21 +857,25 @@
             )
             total = term if b == 0 else total + term
         low = total.astype(BF)
-        for s in range(TILE // piece):
+        piece = TILE // c
+        for d in range(c):
             for p in range(3):
-                r.wq_send[t * (TILE // piece) + s, p] = low[
-                    s * piece : (s + 1) * piece, p * own : (p + 1) * own
+                spread.send_buf[d, p] = low[
+                    d * piece : (d + 1) * piece, p * own : (p + 1) * own
                 ]
-    q_spread.scatter()
-    last_loads = load_qkv(0)
-    for load in last_loads:
-        load.start()
-
-    g_chain.finish()
-    x_chain.finish()
+        spread.scatter()
+
+    for copy in p_copies:
+        copy.wait()
+    for t in range(width // TILE):
+        cols = slice(t * TILE, (t + 1) * TILE)
+        r.block_out[:, cols] = (
+            r.hidden[:, cols] + dot(r.place[...], flat(r.p_recv[:, :, cols]), TN)
+        ).astype(BF)
+
 
     def slab_loads(q):
-        at = lax.rem(grp + q, c)
+        at = partner(grp, q, c)
         base = (q % 2) * width
         out = []
         for which, src in enumerate((r.x_all, r.g_all)):
@@ -786,13 +889,16 @@
                 )
         return out
 
+    def slab_start(q):
+        g_line.wait(partner(grp, q, c))
+        x_line.wait(partner(grp, q, c))
+        for load in slab_loads(q):
+            load.start()
+
     def slab(q):
         base = (q % 2) * width
         for load in slab_loads(q):
             load.wait()
-        if q + 1 < c:
-            for load in slab_loads(q + 1):
-                load.start()
         x_rows, g_rows = r.space.at[pl.ds(base, slots), :], r.space.at[pl.ds(base + slots, slots), :]
 
         def activate(out):
@@ -811,17 +917,34 @@
             3 * width, lambda cols: x_rows[:, cols], lambda cols: g_rows[:, cols], False
         )
 
-    for load in slab_loads(1):
+    slab_start(1)
+
+    slab(1)
+
+    q_spreads[0].total()
+
+    for k in order:
+        to_owner(k).wait()
+    total = wo_rows(r.grad_pre, 0)[...].astype(F32)
+    for e in range(1, n):
+        total = total + wo_rows(r.grad_pre, e)[...].astype(F32)
+    for d in range(c):
+        r.wo_send[d] = total[:, d * (width // c) : (d + 1) * (width // c)].astype(BF)
+    o_spread.scatter()
+    last_loads = load_qkv(0)
+    for load in last_loads:
         load.start()
-    o_spread.total()
-    slab(1)
-    q_spread.total()
+
+    for spread in q_spreads[1:]:
+        spread.total()
+    x_line.hand_on()
 
     for p in (1, 2, 0):
         for t in range(1, n):
             back_home(p, t).wait_recv()
     for load in last_loads:
         load.wait()
+
     for p in range(3):
         for e in range(n):
             r.attended[:, e * own : (e + 1) * own] = r.grad_tok[p, e]
@@ -852,15 +975,37 @@
     for k in order:
         small_ep(k).start()
     r.small_ep[me] = r.small_own[...]
+
+    q_spreads[0].over()
+
+    o_spread.total()
+    if c > 2:
+        slab_start(2)
+        slab(2)
+
+    for spread in q_spreads[1:]:
+        spread.over()
+    q_spreads[0].gather.middle()
     o_spread.over()
-    for q in range(2, c):
+
+    for q in range(3, c):
+        slab_start(q)
+
         slab(q)
-        if q == 2:
-            q_spread.over()
-            o_spread.share()
-    if c <= 2:
-        q_spread.over()
-        o_spread.share()
+
+    out_copies = []
+    for at, (src, dst) in enumerate(((r.sum_in, r.grad_in), (r.sum_out, r.grad_out))):
+        base = at * width
+        for s in range(0, part, CHUNK * 4):
+            r.space[base + s : base + s + CHUNK * 4, :] = src[s : s + CHUNK * 4, :].astype(BF)
+        out_copies.append(
+            pltpu.make_async_copy(
+                r.space.at[pl.ds(base, part), :], dst, r.load_sem.at[at]
+            )
+        )
+    for copy in out_copies:
+        copy.start()
+
     for k in order:
         small_ep(k).wait()
     total = r.small_ep[0]
@@ -870,15 +1015,25 @@
     for t in range(1, c):
         small_dp(t).start()
     r.small_dp[grp] = total
-    q_spread.share()
+
+    spreads = q_spreads + [o_spread]
+    for spread in spreads[1:]:
+        spread.gather.middle()
+    for spread in spreads:
+        spread.gather.last()
+
     for t in range(1, c):
         small_dp(t).wait()
     total = r.small_dp[0]
     for d in range(1, c):
         total = total + r.small_dp[d]
     r.small[...] = total
-    o_spread.finish()
-    q_spread.finish()
+    g_line.finish()
+    x_line.finish()
+    for copy in out_copies:
+        copy.wait()
+    for spread in spreads:
+        spread.finish()
     for p in range(3):
         for t in range(1, n):
             back_home(p, t).wait_send()
@@ -901,8 +1056,8 @@
         q_all=((3, n, width, own), BF, hb),
         o_all=((width, width), BF, hb),
         small=((SMALL, width), F32, vm),
-        grad_in=((part, width), F32, vm),
-        grad_out=((part, width), F32, vm),
+        grad_in=((part, width), BF, hb),
+        grad_out=((part, width), BF, hb),
         g_all=((c, n, cap, width), BF, hb),
         x_all=((c, n, cap, width), BF, hb),
         normed_all=((n, rows, width), BF, hb),
@@ -919,6 +1074,7 @@
 
     heads_shape = (n, rows, own)
     scratch = dict(
+        sum_in=f(part, width), sum_out=f(part, width),
         w_o_v=v(width, width), w_in_v=v(hidden, width), w_out_v=v(hidden, width),
         act=v(slots, hidden), grad_pre=v(slots, hidden), space=v(2 * width, width),
         normed=v(rows, width), place=v(slots, rows), hidden=f(rows, width),
@@ -930,24 +1086,29 @@
         g_send=v(n, cap, width), x_send=v(n, cap, width), g_own=v(n, cap, width),
         x_own=v(n, cap, width), r_recv=v(n, cap, width), p_recv=v(n, cap, width),
         wo_send=v(c, own, piece), wo_recv=v(c, own, piece), wo_fin=v(own, piece),
-        wq_send=v(c, 3, piece, own), wq_recv=v(c, 3, piece, own),
-        wq_fin=v(3, piece, own),
         small_own=f(SMALL, width), small_ep=f(n, SMALL, width), small_sum=f(SMALL, width),
         small_dp=f(c, SMALL, width),
         load_sem=d(8), slab_sem=d(2, 2 * n),
-        a_ss=d(3, n), a_rs=d(3, n), g_ss=d(n), g_rs=d(n), n_ss=d(n), n_rs=d(n),
+        a_ss=d(3, n), a_rs=d(3, n), g_ss=d(n), g_rs=d(n), n_ss=d(n + 2), n_rs=d(n + 2),
         o_ss=d(n), o_rs=d(n), x_ss=d(n), x_rs=d(n), r_ss=d(n), r_rs=d(n), p_ss=d(n), p_rs=d(n),
         b_ss=d(n), b_rs=d(n), w_ss=d(n), w_rs=d(n), d_ss=d(3, n), d_rs=d(3, n),
-        gz_ss=d(2, c), gz_rs=d(2, c), xz_ss=d(2, c), xz_rs=d(2, c),
-        wo_ss=d(2, c), wo_rs=d(2, c), wo_ys=d(n), wo_yr=d(n),
-        wq_ss=d(2, c), wq_rs=d(2, c), wq_ys=d(n), wq_yr=d(n),
+        gz_ss=d(2, c), gz_rs=d(c), xz_ss=d(2, c), xz_rs=d(c),
+        wo_ss=d(2, c), wo_rs=d(2, c), wo_ys=d(n + 2), wo_yr=d(n + 2), wo_ls=d(1),
         s_ss=d(2, max(n, c)), s_rs=d(2, max(n, c)),
     )
+    for t in range(width // TILE):
+        name = "wq" + str(t)
+        piece = TILE // c
+        scratch[name + "_send"] = scratch[name + "_recv"] = v(c, 3, piece, own)
+        scratch[name + "_fin"] = v(3, piece, own)
+        scratch[name + "_ss"] = scratch[name + "_rs"] = d(2, c)
+        scratch[name + "_ys"] = scratch[name + "_yr"] = d(n + 2)
+        scratch[name + "_ls"] = d(1)
     names = list(inputs) + list(outputs) + list(scratch)
 
     def kernel(*refs):
         r = types.SimpleNamespace(**dict(zip(names, refs)))
-        r.heads, r.wo_slot, r.wq_slot = heads, 6, 7
+        r.heads = heads
         block_kernel(r, n, c)
 
     result = pl.pallas_call(
@@ -964,6 +1125,54 @@
 
 
 VMEM_LIMIT = 64 << 20
+STEPS = 8
+
+
+def widen_kernel(q_all, o_all, grad_in, grad_out, block, tokens, small, *outs):
+    q_out, o_out, in_out, out_out, block_out, tokens_out = outs[:6]
+    _, n, _, own = q_all.shape
+    for p in range(3):
+        for e in range(n):
+            at = (p * n + e) * own
+            q_out[:, at : at + own] = q_all[p, e].astype(F32)
+    o_out[...] = o_all[...].astype(F32)
+    in_out[0] = grad_in[...].astype(F32)
+    out_out[0] = grad_out[...].astype(F32)
+    block_out[...] = block[...]
+    tokens_out[...] = tokens[...]
+    for at, one in enumerate(outs[6:]):
+        one[...] = small[at : at + 1, :]
+
+
+def widen(out):
+    q_all, o_all, grad_in, block = out["q_all"], out["o_all"], out["grad_in"], out["block_out"]
+    _, n, width, own = q_all.shape
+    part, rows = grad_in.shape[0], block.shape[0]
+    S = jax.ShapeDtypeStruct
+
+    def rowwise(count):
+        return pl.BlockSpec((count // STEPS, width), lambda i: (i, 0))
+
+    expert = pl.BlockSpec((1, part // STEPS, width), lambda i: (0, i, 0))
+    fixed = pl.BlockSpec((1, width), lambda i: (0, 0))
+    return pl.pallas_call(
+        widen_kernel,
+        grid=(STEPS,),
+        out_shape=[
+            S((width, 3 * width), F32), S((width, width), F32), S((1, part, width), F32),
+            S((1, part, width), F32), S((rows, width), BF), S((rows, width), F32),
+        ] + [S((1, width), F32)] * 4,
+        in_specs=[
+            pl.BlockSpec((3, n, width // STEPS, own), lambda i: (0, 0, i, 0)),
+            rowwise(width), rowwise(part), rowwise(part), rowwise(rows), rowwise(rows),
+            pl.BlockSpec((SMALL, width), lambda i: (0, 0)),
+        ],
+        out_specs=[
+            pl.BlockSpec((width // STEPS, 3 * width), lambda i: (i, 0)),
+            rowwise(width), expert, expert, rowwise(rows), rowwise(rows),
+        ] + [fixed] * 4,
+        compiler_params=pltpu.CompilerParams(vmem_limit_bytes=VMEM_LIMIT),
+    )(q_all, o_all, grad_in, out["grad_out"], block, out["grad_tokens"], out["small"])
 
 
 def on_device(
@@ -997,21 +1206,9 @@
         w_out=w_out,
     )
     out = block_call(n, c, HEADS // n, operands)
-    grad_w_qkv = out["q_all"].transpose(2, 0, 1, 3).reshape(width, 3 * width).astype(F32)
-    grad_w_o = out["o_all"].astype(F32)
-    small = out["small"]
-    return (
-        out["block_out"],
-        out["grad_tokens"],
-        grad_w_qkv,
-        grad_w_o,
-        small[0],
-        small[1],
-        small[2],
-        small[3],
-        out["grad_in"][None],
-        out["grad_out"][None],
-    )
+    q_out, o_out, in_out, out_out, block, tokens_out, *small = widen(out)
+    small = [one.reshape(width) for one in small]
+    return (block, tokens_out, q_out, o_out, *small, in_out, out_out)
 
 
 def solution(mesh):

time: 335 us -> 258 us (0.77); the launches traced: 331 us -> 258 us
  local copies, waits for them, and re-layouts: 34.3 us -> 0 us
  Pallas kernels: 284 us -> 257 us
  other arithmetic: 11.6 us -> 0 us
    pallas_call x1, Pallas kernels: 284 us -> 242 us  [block_call(): pl.pallas_call(kernel, out_shape=[jax.ShapeDtypeStruct(shape, kind) for s...]
    unnamed x15 -> x0, local copies, waits for them, and re-layouts: 20.2 us -> none
    pallas_call x0 -> x1, Pallas kernels: none -> 15.2 us  [widen(): pl.pallas_call(widen_kernel, grid=(STEPS,), out_shape=[S((width, 3 * widt...]
    convert_element_type x1 -> x0, local copies, waits for them, and re-layouts: 12.5 us -> none  [on_device(): out['q_all'].transpose(2, 0, 1, 3).reshape(width, 3 * width).astype(F32)]
    convert_element_type x2 -> x0, other arithmetic: 11.6 us -> none  [the longest x1 9 us: on_device(): out['q_all'].transpose(2, 0, 1, 3).reshape(width, 3 * width).astype(F32)]
where the time goes in v3:
time: 258 us
  Pallas kernels  257 us (100%)
    pallas_call x1, Pallas kernels, block_call(): pl.pallas_call(kernel, out_shape=[jax.ShapeDtypeStruct(shape, kind) for s...  242 us
    pallas_call x1, Pallas kernels, widen(): pl.pallas_call(widen_kernel, grid=(STEPS,), out_shape=[S((width, 3 * widt...  15.2 us

profile of v3, /device:TPU:0, one launch (start us, length us, event | category | flops | bytes accessed | tf_op | source)
XLA Modules:
  0.0 257.9 jit_solution(18329721968626410871)
XLA Ops:
  0.6 241.9 %shard_map.195 = (bf16[256,1024]{1,0:T(8,128)(2,1)}, f32[256,1024]{1,0:T(8,128)}, bf16[3,8,1024,128]{3,2,1,0:T(8,128)(2,1)}, bf16[1024,1024]{1,0:T(8,128)(2,1)},...) custom-call(s32[1,4]{1,0:T(1,128)} %refs_0_.1, ...), custom_call_target="tpu_custom_call" | custom-call | tf_op jit(solution)/shard_map/pallas_call | solution.py:1114
  242.5 15.2 %shard_map.196 = (f32[1024,3072]{1,0:T(8,128)}, f32[1024,1024]{1,0:T(8,128)}, f32[1,1024,1024]{2,1,0:T(8,128)}, f32[1,1024,1024]{2,1,0:T(8,128)}, bf16[256,1024]...) custom-call(bf16[3,8,1024,128]{3,2,1,0:T(8,128)(2,1)} %get-tuple-ele, ...), custom_call_target="tpu_custom_call" | custom-call | tf_op jit(solution)/shard_map/pallas_call | solution.py:1158

commit v4 on v3

--- a/solution.py
+++ b/solution.py
@@ -55,9 +55,11 @@
     return value.reshape(value.shape[0] * value.shape[1], value.shape[2])
 
 
-def tiles(count, body):
+def tiles(count, body, beside=None):
     def step(t, _):
         body(pl.ds(pl.multiple_of(t * TILE, TILE), TILE))
+        for at, act in (beside or {}).items():
+            pl.when(t == at)(act)
         return 0
 
     lax.fori_loop(0, count // TILE, step, 0)
@@ -282,11 +284,14 @@
 
 
 class Line:
-    def __init__(self, block, whole, send_sem, recv_sem, at, c):
+    def __init__(self, block, whole, send_sem, recv_sem, at, c, hops):
         self.block, self.whole, self.at, self.c = block, whole, at, c
-        self.send_sem, self.recv_sem = send_sem, recv_sem
-
-    def direct(self, way, hops):
+        self.send_sem, self.recv_sem, self.hops = send_sem, recv_sem, min(hops, c - 1)
+
+    def can(self, index):
+        return (index >= 0) & (index < self.c)
+
+    def first(self, way, hops):
         target = self.at + way * hops
         return self.can(target), send(
             self.block,
@@ -296,41 +301,38 @@
             {"dp": target},
         )
 
-    def can(self, index):
-        return (index >= 0) & (index < self.c)
-
     def onward(self, way, stage):
-        held = self.at - way * (2 + stage)
-        target = self.at + way
+        held, target = self.at - way * (self.hops - 1 + stage), self.at + way
         src = self.whole.at[held]
         return self.can(held) & self.can(target), send(
             src,
             src,
-            self.send_sem.at[(way + 1) // 2, 2 + stage],
+            self.send_sem.at[(way + 1) // 2, self.hops - 1 + stage],
             self.recv_sem.at[held],
             {"dp": target},
         )
 
     def start(self):
-        for hops in range(1, min(3, self.c)):
+        for hops in range(1, self.hops + 1):
             for way in (-1, 1):
-                allowed, copy = self.direct(way, hops)
+                allowed, copy = self.first(way, hops)
                 pl.when(allowed)(copy.start)
 
-    def hand_on(self):
-        for stage in range(self.c - 3):
-            for way in (-1, 1):
-                allowed, copy = self.onward(way, stage)
-
-                @pl.when(allowed)
-                def _():
-                    copy.wait_recv()
-                    copy.start()
+    def hand_on(self, *stages):
+        for stage in stages:
+            if stage < self.c - self.hops:
+                for way in (-1, 1):
+                    allowed, copy = self.onward(way, stage)
+
+                    @pl.when(allowed)
+                    def _():
+                        copy.wait_recv()
+                        copy.start()
 
     def wait(self, block):
-        away = block - self.at
-        below, above = away < -1, away > 1
-        done = (below & self.can(self.at + 1)) | (above & self.can(self.at - 1))
+        done = ((block <= self.at - self.hops) & self.can(self.at + 1)) | (
+            (block >= self.at + self.hops) & self.can(self.at - 1)
+        )
 
         @pl.when(jnp.logical_not(done))
         def _():
@@ -339,10 +341,10 @@
 
     def finish(self):
         for way in (-1, 1):
-            for hops in range(1, min(3, self.c)):
-                allowed, copy = self.direct(way, hops)
+            for hops in range(1, self.hops + 1):
+                allowed, copy = self.first(way, hops)
                 pl.when(allowed)(copy.wait_send)
-            for stage in range(self.c - 3):
+            for stage in range(1, self.c - self.hops):
                 allowed, copy = self.onward(way, stage)
                 pl.when(allowed)(copy.wait_send)
 
@@ -471,7 +473,7 @@
     part = hidden // c
     order = order_of(n)
     direct = [k for k in order if k % 2 == 0]
-    partners = {k: partner(me, k, n) for k in order}
+    partners = {k: partner(me, k, n) for k in range(n)}
     half = width // 2
 
     def to_partner(src, dst, send_sem, recv_sem, k):
@@ -542,8 +544,8 @@
             to_heads(p, k).start()
         r.qkv_heads[p, me] = r.qkv_send[p, me]
 
-    g_line = Line(r.g_own, r.g_all, r.gz_ss, r.gz_rs, grp, c)
-    x_line = Line(r.x_own, r.x_all, r.xz_ss, r.xz_rs, grp, c)
+    g_line = Line(r.g_own, r.g_all, r.gz_ss, r.gz_rs, grp, c, 1)
+    x_line = Line(r.x_own, r.x_all, r.xz_ss, r.xz_rs, grp, c, 1)
     for copy in g_copies:
         copy.wait()
     g_line.start()
@@ -590,6 +592,7 @@
         def _():
             home(t).start()
 
+        pl.when(t == n // 2)(lambda: g_line.hand_on(1))
         return 0
 
     lax.fori_loop(0, n, block_step, 0)
@@ -621,7 +624,6 @@
         r.grad_pre[:, cols] = dot(flat(r.g_own[...]), r.w_out_v[cols, :], NT).astype(BF)
 
     tiles(hidden, act_grad)
-    g_line.hand_on()
     load_in.wait()
 
     for copy in x_copies:
@@ -637,7 +639,7 @@
             r.act[at, cols] = act.astype(BF)
             r.grad_pre[at, cols] = (r.grad_pre[at, cols].astype(F32) * slope).astype(BF)
 
-    tiles(hidden, expert_step)
+    tiles(hidden, expert_step, {2: lambda: g_line.hand_on(2)})
 
     def routed_grad(cols):
         r.g_send[:, :, cols] = (
@@ -683,7 +685,8 @@
     for copy in r_copies:
         copy.wait()
 
-    normed_gather.middle()
+    x_line.hand_on(1)
+    g_line.hand_on(*range(3, c))
 
     for t in range(width // TILE):
         cols = slice(t * TILE, (t + 1) * TILE)
@@ -719,19 +722,41 @@
             r.attended[:, out], r.block_out[...], TN
         ).astype(BF)
 
+    def to_sibling(k):
+        at = partners[k]
+        return to_partner(
+            wo_rows(r.act, at), wo_rows(r.grad_pre, at), r.w_ss.at[k], r.w_rs.at[k], 1
+        )
+
     def to_owner(k):
         return to_partner(
-            wo_rows(r.act, partners[k]), wo_rows(r.grad_pre, me), r.w_ss.at[k], r.w_rs.at[k], k
+            wo_rows(r.act, partners[k]),
+            wo_rows(r.grad_pre, partners[1]),
+            r.w_ss.at[k],
+            r.w_rs.at[k],
+            k,
         )
 
     for copy in a_copies:
         copy.wait()
+    normed_gather.middle()
     p_copies = [blocks_out(r.x_send, r.p_recv, (r.p_ss, r.p_rs), k) for k in order]
     for copy in p_copies:
         copy.start()
-    for k in order:
-        to_owner(k).start()
-    wo_rows(r.grad_pre, me)[...] = wo_rows(r.act, me)[...]
+
+    for k in range(1, n, 2):
+        to_sibling(k).start()
+
+    def wo_across():
+        for k in range(1, n, 2):
+            to_sibling(k).wait()
+        for k in [0] + direct:
+            mine_k = wo_rows(r.act, partners[k])
+            mine_k[...] = (
+                mine_k[...].astype(F32) + wo_rows(r.grad_pre, partners[k])[...].astype(F32)
+            ).astype(BF)
+        for k in direct:
+            to_owner(k).start()
 
     for p in range(3):
         for k in order:
@@ -761,6 +786,7 @@
 
     def back_step(t, _):
         attend_back(r, lax.rem(me + t, n), n)
+        pl.when(t == 0)(wo_across)
 
         @pl.when(t > 0)
         def _():
@@ -921,13 +947,11 @@
 
     slab(1)
 
-    q_spreads[0].total()
-
-    for k in order:
+    for k in direct:
         to_owner(k).wait()
-    total = wo_rows(r.grad_pre, 0)[...].astype(F32)
-    for e in range(1, n):
-        total = total + wo_rows(r.grad_pre, e)[...].astype(F32)
+    total = wo_rows(r.act, me)[...].astype(F32)
+    for k in direct:
+        total = total + wo_rows(r.grad_pre, partners[k + 1])[...].astype(F32)
     for d in range(c):
         r.wo_send[d] = total[:, d * (width // c) : (d + 1) * (width // c)].astype(BF)
     o_spread.scatter()
@@ -935,9 +959,9 @@
     for load in last_loads:
         load.start()
 
-    for spread in q_spreads[1:]:
+    for spread in q_spreads:
         spread.total()
-    x_line.hand_on()
+    x_line.hand_on(*range(2, c))
 
     for p in (1, 2, 0):
         for t in range(1, n):
@@ -976,9 +1000,9 @@
         small_ep(k).start()
     r.small_ep[me] = r.small_own[...]
 
+    o_spread.total()
     q_spreads[0].over()
 
-    o_spread.total()
     if c > 2:
         slab_start(2)
         slab(2)
@@ -1125,7 +1149,7 @@
 
 
 VMEM_LIMIT = 64 << 20
-STEPS = 8
+STEPS = 4
 
 
 def widen_kernel(q_all, o_all, grad_in, grad_out, block, tokens, small, *outs):

time: 258 us -> 241 us (0.934)
  Pallas kernels: 257 us -> 239 us
    pallas_call x1, Pallas kernels: 242 us -> 225 us  [block_call(): pl.pallas_call(kernel, out_shape=[jax.ShapeDtypeStruct(shape, kind) for s...]
where the time goes in v4:
time: 241 us; the launch traced here: 240 us
  Pallas kernels  239 us (99%)
    pallas_call x1, Pallas kernels, block_call(): pl.pallas_call(kernel, out_shape=[jax.ShapeDtypeStruct(shape, kind) for s...  225 us
    pallas_call x1, Pallas kernels, widen(): pl.pallas_call(widen_kernel, grid=(STEPS,), out_shape=[S((width, 3 * widt...  13.9 us

profile of v4, /device:TPU:0, one launch (start us, length us, event | category | flops | bytes accessed | tf_op | source)
XLA Modules:
  0.0 239.9 jit_solution(11590223477482540082)
XLA Ops:
  0.6 225.2 %shard_map.195 = (bf16[256,1024]{1,0:T(8,128)(2,1)}, f32[256,1024]{1,0:T(8,128)}, bf16[3,8,1024,128]{3,2,1,0:T(8,128)(2,1)}, bf16[1024,1024]{1,0:T(8,128)(2,1)},...) custom-call(s32[1,4]{1,0:T(1,128)} %refs_0_.1, ...), custom_call_target="tpu_custom_call" | custom-call | tf_op jit(solution)/shard_map/pallas_call | solution.py:1138
  225.8 13.9 %shard_map.196 = (f32[1024,3072]{1,0:T(8,128)}, f32[1024,1024]{1,0:T(8,128)}, f32[1,1024,1024]{2,1,0:T(8,128)}, f32[1,1024,1024]{2,1,0:T(8,128)}, bf16[256,1024]...) custom-call(bf16[3,8,1024,128]{3,2,1,0:T(8,128)(2,1)} %get-tuple-ele, ...), custom_call_target="tpu_custom_call" | custom-call | tf_op jit(solution)/shard_map/pallas_call | solution.py:1182
